TPU v7x, 256 devices: a whole 4x4x8 slice. The times are simulated.
256 devices in a mesh: batch: 8 (over x_hi, y), prefix: 32 (over z, x_lo, core).
Axes of the slice: x: 4 (x_hi: 2, x_lo: 2; x = x_hi * 2 + x_lo), y: 4, z: 8, core: 2. Of those that a mesh axis runs over, the one named last changes fastest.
Arguments:
- queries: bfloat16 [32, 128, 8192], P('batch', None, 'prefix'), may hold values from -32 to 32
- prompt_key_cache: bfloat16 [16384, 1024], P('prefix'), may hold values from -10 to 10
- prompt_value_cache: bfloat16 [16384, 1024], P('prefix'), may hold values from -12 to 12
- response_keys: bfloat16 [32, 128, 1024], P('batch'), may hold values from -10 to 10
- response_values: bfloat16 [32, 128, 1024], P('batch'), may hold values from -12 to 12
- lengths: int32 [32], P('batch'), may hold values from 32 to 128, as said below
- out_weight: bfloat16 [8192, 5120], P('prefix', 'batch'), may hold values from -0.0625 to 0.0625
Outputs:
- scored: bfloat16 [4096, 5120], P(('batch', 'prefix'))
Inputs may be any that keep to these rules, and one draw needn't show every extreme that they name: `lengths`: some response in every draw has all 128 tokens valid.
All inputs are finite; a program needn't handle non-finite values.
Results may differ from a plain program's by a relative error of at most 0.0052.
Values may be sent and summed in bfloat16 or wider, within the bound.
No kernel may reach another device: no remote copies, remote signals or barrier semaphores. Data moves between devices by JAX's collectives and lax.ppermute only.
A program may use at most 128 MiB of HBM per device.

v0:
```python
import functools
import math

import jax
import jax.numpy as jnp
from jax import lax
from jax.experimental import pallas as pl
from jax.experimental.pallas import tpu as pltpu
from jax.sharding import Mesh, PartitionSpec as P

HEAD_SIZE = 128
LANES = 128
F32 = jnp.float32
BF16 = jnp.bfloat16
SCORE_SCALE = HEAD_SIZE**-0.5 * math.log2(math.e)
LOWEST = -1e30
VMEM_LIMIT = 24 * 2**20
SUB_AXES = ("xh", "y", "z", "xl", "c")
PREFIX = ("z", "xl", "c")
SWAP = [(0, 1), (1, 0)]
PARTS = 2
SLAB = 8
SLOTS = 4
STAT_ROWS = 16
CHUNK = 256
FLOPS_PER_MICRO = 1.15e9


def score_dot(q, k):
    return lax.dot_general(q, k, (((1,), (1,)), ((), ())), preferred_element_type=F32)


def absorb(state, scores, values):
    top, total, acc = state
    new_top = jnp.maximum(top, scores.max(-1, keepdims=True) * SCORE_SCALE)
    decay = jnp.exp2(top - new_top)
    weights = jnp.exp2(scores * SCORE_SCALE - new_top).astype(BF16)
    extended = jnp.concatenate([values, jnp.ones(values.shape, BF16)], axis=1)
    added = jnp.dot(weights, extended, preferred_element_type=F32)
    return new_top, total * decay + added[:, 128:129], acc * decay + added[:, :128]


def empty_state(rows):
    return (
        jnp.full((rows, 1), LOWEST, F32),
        jnp.zeros((rows, 1), F32),
        jnp.zeros((rows, HEAD_SIZE), F32),
    )


def store_state(state, acc_out, stat_out):
    top, total, acc = state
    acc_out[...] = acc
    lane = lax.broadcasted_iota(jnp.int32, acc.shape, 1)
    stat_out[...] = jnp.where(lane < 64, top, total)


def load_state(acc_in, stat_in):
    stat = stat_in[...]
    lane = lax.broadcasted_iota(jnp.int32, stat.shape, 1)
    top = jnp.where(lane < 64, stat, LOWEST).max(-1, keepdims=True)
    total = jnp.where(lane < 64, 0.0, stat).max(-1, keepdims=True)
    return top, total, acc_in[...]


def absorb_block(state, q, keys, values, chunk=CHUNK):
    count = keys.shape[0]
    for at in range(0, count, chunk):
        to = min(at + chunk, count)
        state = absorb(state, score_dot(q, keys[at:to, :]), values[at:to, :])
    return state


def first_own_kernel(q_ref, rk_ref, rv_ref, block, acc_out, stat_out):
    count, resp_len, _ = rk_ref.shape
    part = resp_len // PARTS
    row = lax.broadcasted_iota(jnp.int32, (part, resp_len), 0)
    col = lax.broadcasted_iota(jnp.int32, (part, resp_len), 1)
    token = (row // SLAB) * (PARTS * SLAB) + pl.program_id(0) * SLAB + row % SLAB
    tops, totals, accs = [], [], []
    for at in range(0, q_ref.shape[0], part):
        r = at // part % count
        scores = score_dot(q_ref[at : at + part, :], rk_ref[r])
        scores = jnp.where(token >= col, scores, LOWEST)
        top, total, acc = absorb(empty_state(part), scores, rv_ref[r])
        tops.append(top)
        totals.append(total)
        accs.append(acc)
    state = tuple(jnp.concatenate(part, axis=0) for part in (tops, totals, accs))
    state = absorb_block(state, q_ref[...], block.at[0], block.at[1], 512)
    store_state(state, acc_out, stat_out)


def first_all_kernel(q_ref, block, near_block, acc_in, stat_in, acc_out, stat_out):
    rows = q_ref.shape[0]
    own_rows = acc_in.shape[0]
    own = pl.program_id(0) % (SLOTS * own_rows // rows) == 0

    def absorb_first(start):
        state = empty_state(rows - start)
        state = absorb_block(state, q_ref[start:, :], block.at[0], block.at[1])
        store_state(state, acc_out.at[start:, :], stat_out.at[start:, :])

    @pl.when(own)
    def _():
        acc_out[:own_rows, :] = acc_in[...]
        stat_out[:own_rows, :] = stat_in[...]
        absorb_first(own_rows)

    @pl.when(jnp.logical_not(own))
    def _():
        absorb_first(0)

    state = load_state(acc_out, stat_out)
    state = absorb_block(state, q_ref[...], near_block.at[0], near_block.at[1])
    store_state(state, acc_out, stat_out)


def middle_kernel(count, q_ref, *refs):
    blocks, (acc_in, stat_in, acc_out, stat_out) = refs[:count], refs[count:]
    state = load_state(acc_in, stat_in)
    for block in blocks:
        state = absorb_block(state, q_ref[...], block.at[0], block.at[1])
    store_state(state, acc_out, stat_out)


def narrow(columns):
    rows = columns.shape[0]
    lines = []
    for at in range(0, rows, LANES):
        wide = jnp.broadcast_to(columns[at : at + LANES], (LANES, LANES))
        lines.append(wide.T[0:1])
    lines.append(jnp.zeros((STAT_ROWS - rows // LANES, LANES), F32))
    return jnp.concatenate(lines, axis=0)


def widen(lines, rows):
    columns = []
    for i in range(rows // LANES):
        columns.append(jnp.broadcast_to(lines[i : i + 1], (LANES, LANES)).T)
    return jnp.concatenate(columns, axis=0)


def store_sent(sent_ref, out, lines):
    rows = out.shape[0]
    sent_ref[0:rows, :] = out.astype(BF16)
    for i in range(3):
        term = lines.astype(BF16)
        sent_ref[rows + i * STAT_ROWS : rows + (i + 1) * STAT_ROWS, :] = term
        lines = lines - term.astype(F32)


def load_sent(sent_ref):
    rows = sent_ref.shape[0] - 3 * STAT_ROWS
    lines = jnp.zeros((STAT_ROWS, LANES), F32)
    for i in range(3):
        term = sent_ref[rows + i * STAT_ROWS : rows + (i + 1) * STAT_ROWS, :]
        lines = lines + term.astype(F32)
    return sent_ref[0:rows, :].astype(F32), widen(lines, rows)


def merge(out_a, lse_a, out_b, lse_b):
    top = jnp.maximum(lse_a, lse_b)
    weight_a, weight_b = jnp.exp2(lse_a - top), jnp.exp2(lse_b - top)
    total = weight_a + weight_b
    return (weight_a * out_a + weight_b * out_b) / total, top + jnp.log2(total)


def finish(q_ref, blocks, acc_in, stat_in):
    state = load_state(acc_in, stat_in)
    keys, values = blocks
    top, total, acc = absorb_block(state, q_ref[...], keys, values)
    return acc / total, top + jnp.log2(total)


def far_kernel(q_ref, acc_in, stat_in, *refs):
    blocks, sent_ref = refs[:-1], refs[-1]
    out, lse = finish(q_ref, blocks, acc_in, stat_in)
    store_sent(sent_ref, out, narrow(lse))


def near_kernel(q_ref, acc_in, stat_in, *refs):
    blocks, (got_ref, out_ref, lines_ref, sent_ref) = refs[:-4], refs[-4:]
    out, lse = finish(q_ref, blocks, acc_in, stat_in)
    out, lse = merge(out, jnp.broadcast_to(lse, out.shape), *load_sent(got_ref))
    lines = narrow(lse[:, 0:1])
    out_ref[...] = out
    lines_ref[...] = lines
    store_sent(sent_ref, out, lines)


def last_merge_kernel(part, lengths_ref, out_ref, lines_ref, got_ref, attended_ref):
    tokens, width = attended_ref.shape
    rows = out_ref.shape[0]
    half = rows // 2
    got, got_lse = load_sent(got_ref)
    got = jnp.concatenate([got[half:], got[:half]], axis=0)
    got_lse = jnp.concatenate([got_lse[half:], got_lse[:half]], axis=0)
    out, _ = merge(out_ref[...], widen(lines_ref[...], rows), got, got_lse)
    row = lax.broadcasted_iota(jnp.int32, (tokens, LANES), 0)
    count = lengths_ref.shape[0]
    per = tokens // count
    token = (row % per) // SLAB * (PARTS * SLAB) + part * SLAB + row % SLAB
    valid = jnp.zeros((tokens, LANES), jnp.int32)
    for r in range(count):
        valid = jnp.where(row // per == r, lengths_ref[r], valid)
    live = token < valid
    for i in range(width // HEAD_SIZE):
        head = jnp.where(live, out[i * tokens : (i + 1) * tokens], 0.0)
        attended_ref[:, i * HEAD_SIZE : (i + 1) * HEAD_SIZE] = head.astype(BF16)


def project_kernel(w_ref, *refs):
    pairs, out_ref = refs[:-1], refs[-1]
    devices, _, rows, width = out_ref.shape
    depth = w_ref.shape[1] // 4
    for part in range(PARTS):
        product = 0.0
        for i in range(4):
            ref, at = pairs[2 * part + i % 2], i // 2 * depth
            weight = w_ref[:, i * depth : (i + 1) * depth]
            product = product + score_dot(ref[:, at : at + depth], weight)
        out_ref[:, part] = product.reshape(devices, rows, width).astype(BF16)


def total_kernel(blocks, xh_ref, *refs):
    parts, out_ref = refs[:-1], refs[-1]
    half = out_ref.shape[1] // 2
    lines = []
    for ref in parts:
        count, rows, columns = ref.shape
        sums = ref[...].astype(F32).reshape(count // SLOTS, SLOTS, rows, columns).sum(0)
        piece = columns // blocks
        turned = []
        for rel in range(2):
            starts = range(rel * piece, columns, 2 * piece)
            pieces = [sums[q][:, at : at + piece] for at in starts for q in range(SLOTS)]
            turned.append(jnp.concatenate(pieces, axis=1))
        lines.append(turned)
    here = jnp.concatenate([line[0] for line in lines], axis=0).astype(BF16)
    there = jnp.concatenate([line[1] for line in lines], axis=0).astype(BF16)
    at_here = pl.multiple_of(xh_ref[0] * half, half)
    at_there = pl.multiple_of((1 - xh_ref[0]) * half, half)
    out_ref[:, pl.ds(at_here, half)] = here
    out_ref[:, pl.ds(at_there, half)] = there


def call(kernel, name, micros, order=(), in_specs=(), **options):
    def run(*operands):
        held = jnp.zeros((1,), jnp.int32)
        if order:
            held = after(held, *order)
        return pl.pallas_call(
            lambda held_ref, *refs: kernel(*refs),
            name=name,
            in_specs=[SMEM, *in_specs],
            cost_estimate=pl.CostEstimate(
                flops=int(micros * FLOPS_PER_MICRO), bytes_accessed=1, transcendentals=0
            ),
            compiler_params=pltpu.CompilerParams(vmem_limit_bytes=VMEM_LIMIT),
            **options,
        )(held, *operands)

    return run


def whole(array):
    return pl.BlockSpec(array.shape, lambda i: (0,) * array.ndim)


def rows_spec(tile, index=lambda i: i):
    return pl.BlockSpec((tile, HEAD_SIZE), lambda i: (index(i), 0))


def shapes_of(arrays):
    return [jax.ShapeDtypeStruct(a.shape, a.dtype) for a in arrays]


VMEM = pl.BlockSpec(memory_space=pltpu.VMEM)
SMEM = pl.BlockSpec(memory_space=pltpu.SMEM)


def first_own(q, resp_k, resp_v, block, order):
    tile = q.shape[0] // PARTS
    state = jax.ShapeDtypeStruct(q.shape, F32)
    return call(
        first_own_kernel,
        "attend_own",
        5,
        order,
        grid=(PARTS,),
        in_specs=[rows_spec(tile), whole(resp_k), whole(resp_v), whole(block)],
        out_specs=[rows_spec(tile)] * 2,
        out_shape=[state] * 2,
    )(q, resp_k, resp_v, block)


def first_all(q, block, near_block, own_state, tile, order):
    own_rows = q.shape[0] // (PARTS * SLOTS)
    state = jax.ShapeDtypeStruct(q.shape, F32)
    tiles = q.shape[0] // tile
    held = rows_spec(own_rows, lambda i: i * PARTS // tiles)
    return call(
        first_all_kernel,
        "attend_first",
        11,
        order,
        grid=(tiles,),
        in_specs=[rows_spec(tile), whole(block), whole(near_block), held, held],
        out_specs=[rows_spec(tile)] * 2,
        out_shape=[state] * 2,
    )(q, block, near_block, *own_state)


def attend_more(q, blocks, state, tile, order, start=0, rows=None):
    rows = rows or q.shape[0]
    count = len(blocks)
    at = start // tile
    moved = rows_spec(tile, lambda i: i + at)
    return call(
        functools.partial(middle_kernel, count),
        "attend_more",
        7 * count * rows // q.shape[0],
        order,
        grid=(rows // tile,),
        in_specs=[moved] + [whole(b) for b in blocks] + [moved] * 2,
        out_specs=[rows_spec(tile)] * 2,
        out_shape=[jax.ShapeDtypeStruct((rows, HEAD_SIZE), F32)] * 2,
    )(q, *blocks, *state)


def attend_far(q, blocks, state, part, rows, order):
    moved = rows_spec(rows, lambda i: 2 * part + 1)
    sent = jax.ShapeDtypeStruct((rows + 3 * STAT_ROWS, HEAD_SIZE), BF16)
    return call(
        far_kernel,
        "attend_far",
        2,
        order,
        grid=(1,),
        in_specs=[moved] * 3 + [whole(b) for b in blocks],
        out_specs=whole(sent),
        out_shape=sent,
    )(q, *state, *blocks)


def attend_near(q, blocks, state, got, part, rows, order):
    moved = rows_spec(rows, lambda i: 2 * part)
    out_shape = [
        jax.ShapeDtypeStruct((rows, HEAD_SIZE), F32),
        jax.ShapeDtypeStruct((STAT_ROWS, LANES), F32),
        jax.ShapeDtypeStruct(got.shape, BF16),
    ]
    return call(
        near_kernel,
        "attend_near",
        2,
        order,
        grid=(1,),
        in_specs=[moved] * 3 + [whole(b) for b in blocks] + [whole(got)],
        out_specs=[whole(s) for s in out_shape],
        out_shape=out_shape,
    )(q, *state, *blocks, got)


def last_merge(part, lengths, out, lines, got, tokens, order):
    attended = jax.ShapeDtypeStruct((tokens, out.shape[0] // tokens * HEAD_SIZE), BF16)
    return call(
        functools.partial(last_merge_kernel, part),
        "merge_last",
        1,
        order,
        grid=(1,),
        in_specs=[SMEM] + [whole(a) for a in (out, lines, got)],
        out_specs=whole(attended),
        out_shape=attended,
    )(lengths, out, lines, got)


def project(pairs, weight, tile=640):
    devices = pairs[0].shape[0] // SLAB
    columns, depth = weight.shape
    return call(
        project_kernel,
        "project",
        3,
        grid=(columns // tile,),
        in_specs=[pl.BlockSpec((tile, depth), lambda i: (i, 0))] + [whole(a) for a in pairs],
        out_specs=pl.BlockSpec((devices, PARTS, SLAB, tile), lambda i: (0, 0, 0, i)),
        out_shape=jax.ShapeDtypeStruct((devices, PARTS, SLAB, columns), BF16),
    )(weight, *pairs)


def add_up(xh, parts, width, blocks):
    rows = sum(part.shape[1] for part in parts)
    out = jax.ShapeDtypeStruct((rows, width), BF16)
    return call(
        functools.partial(total_kernel, blocks),
        "add_up",
        2,
        grid=(1,),
        in_specs=[SMEM] + [whole(p) for p in parts],
        out_specs=whole(out),
        out_shape=out,
    )(xh.reshape(1), *parts)


def pack_kernel(z_ref, y_ref, k_ref, v_ref, own_ref, sent_ref):
    groups, _, count, _ = sent_ref.shape
    here = pl.ds(pl.multiple_of(z_ref[0] * HEAD_SIZE, HEAD_SIZE), HEAD_SIZE)
    own_ref[0] = k_ref[:, here]
    own_ref[1] = v_ref[:, here]
    rows = pl.ds(pl.multiple_of(y_ref[0] * count, count), count)
    for group in range(groups):
        columns = slice(group * HEAD_SIZE, (group + 1) * HEAD_SIZE)
        sent_ref[group, 0] = k_ref[rows, columns]
        sent_ref[group, 1] = v_ref[rows, columns]


def pack(z, y, y_size, keys, values):
    groups = keys.shape[1] // HEAD_SIZE
    count = keys.shape[0]
    out_shape = [
        jax.ShapeDtypeStruct((2, count, HEAD_SIZE), BF16),
        jax.ShapeDtypeStruct((groups, 2, count // y_size, HEAD_SIZE), BF16),
    ]
    return call(
        pack_kernel,
        "pack_heads",
        2,
        grid=(1,),
        in_specs=[SMEM] * 2 + [whole(keys), whole(values)],
        out_specs=[whole(s) for s in out_shape],
        out_shape=out_shape,
    )(z.reshape(1), y.reshape(1), keys, values)


def unpack_kernel(z_ref, got_ref, out_ref):
    groups, _, count, _ = got_ref.shape
    for i in range(groups - 1):
        source = lax.rem(z_ref[0] + 1 + i, groups)
        out_ref[0, i * count : (i + 1) * count] = got_ref[source, 0]
        out_ref[1, i * count : (i + 1) * count] = got_ref[source, 1]


def unpack(z, got):
    groups, two, count, width = got.shape
    out = jax.ShapeDtypeStruct((two, (groups - 1) * count, width), BF16)
    return call(
        unpack_kernel,
        "unpack_heads",
        1,
        grid=(1,),
        in_specs=[SMEM, whole(got)],
        out_specs=whole(out),
        out_shape=out,
    )(z.reshape(1), got)


def after(array, *others):
    return lax.optimization_barrier((array, *others))[0]


def weight_of_core(out_weight, c):
    depth, width = out_weight.shape
    quarters = out_weight.T.reshape(2, 2, width // 4, depth)
    of_c = lax.dynamic_index_in_dim(quarters, c, 1, keepdims=False)
    sent = lax.dynamic_index_in_dim(quarters, 1 - c, 1, keepdims=False)
    return jnp.concatenate([of_c, lax.ppermute(sent, "c", SWAP)], axis=2)


def on_device(queries, keys, values, resp_keys, resp_values, lengths, out_weight):
    xh, y, z, xl, c = (lax.axis_index(a) for a in SUB_AXES)
    resp_count, resp_len, features = queries.shape
    tokens = resp_count * resp_len
    y_size = lax.axis_size("y")
    own_heads = features // HEAD_SIZE
    part_tokens = tokens // PARTS
    slot_rows = own_heads * part_tokens
    width = out_weight.shape[1]

    both = weight_of_core(out_weight, c)
    w_own = lax.dynamic_index_in_dim(both, xl, 0, keepdims=False)
    w_sent = lax.dynamic_index_in_dim(both, 1 - xl, 0, keepdims=False)
    w_x = lax.ppermute(w_sent, "xl", SWAP)
    w_h = lax.ppermute(w_own, "xh", SWAP)
    w_xh = lax.ppermute(w_sent, ("xh", "xl"), [(i, 3 - i) for i in range(4)])
    own_block, sent = pack(z, y, y_size, keys, values)
    got = lax.all_to_all(after(sent, both), "z", split_axis=0, concat_axis=0, tiled=True)

    q_own = after(queries, own_block).reshape(-1, PARTS, SLAB, own_heads, HEAD_SIZE)
    q_own = q_own.transpose(1, 3, 0, 2, 4).reshape(PARTS * slot_rows, HEAD_SIZE)
    q_every = lax.all_gather(q_own, ("xl", "c"), axis=0, tiled=False)

    up = [(i, (i + 1) % y_size) for i in range(y_size)]
    down = [(i, (i - 1) % y_size) for i in range(y_size)]
    head = z * HEAD_SIZE
    rk = lax.dynamic_slice_in_dim(resp_keys, head, HEAD_SIZE, 2)
    rv = lax.dynamic_slice_in_dim(resp_values, head, HEAD_SIZE, 2)
    state = first_own(q_own, rk, rv, own_block, (w_x, w_h, w_xh))
    near_y = unpack(z, after(got, state[0]))
    from_below = lax.ppermute(near_y, "y", up)
    from_above = lax.ppermute(near_y, "y", down)
    here = jnp.concatenate([w_own, w_x], axis=1)
    there = jnp.concatenate([w_h, w_xh], axis=1)
    weight = lax.all_gather(jnp.concatenate([here, there], axis=0), "y", axis=0, tiled=True)

    q_every = after(q_every, state[0])
    mine = 2 * xl + c
    slots = [q_own] + [
        lax.dynamic_index_in_dim(q_every, mine ^ i, 0, keepdims=False) for i in (2, 1, 3)
    ]
    slots = [q.reshape(PARTS, 1, slot_rows, HEAD_SIZE) for q in slots]
    q_all = jnp.concatenate(slots, axis=1).reshape(-1, HEAD_SIZE)
    state = first_all(q_all, own_block, near_y, state, 1024, ())
    far_k = lax.ppermute(after(from_below, state[0])[0], "y", up)
    far_v = lax.ppermute(after(from_above, state[0])[1], "y", down)
    state = attend_more(q_all, [from_below, from_above], state, 1024, ())
    half = 2 * slot_rows
    blocks = [far_k, far_v]
    far = []
    for part in range(PARTS):
        order = (far[-1],) if far else ()
        far.append(attend_far(q_all, blocks, state, part, half, order))
    far_c = [lax.ppermute(f, "c", SWAP) for f in far]
    near, near_x, merged = [], [], []
    for part in range(PARTS):
        order = (near[-1][0],) if near else (far[-1],)
        out, lines, sent = attend_near(q_all, blocks, state, far_c[part], part, half, order)
        near.append((out, lines))
        near_x.append(lax.ppermute(sent, "xl", SWAP))
    for part in range(PARTS - 1):
        merged.append(
            last_merge(part, lengths, *near[part], near_x[part], part_tokens, (near[-1][0], weight))
        )
    merged.append(
        last_merge(PARTS - 1, lengths, *near[-1], near_x[-1], part_tokens, (merged[-1],))
    )
    pairs = []
    for attended in merged:
        pairs += [attended, lax.ppermute(attended, "c", SWAP)]
    partial = project(pairs, weight)
    partial = partial.reshape(partial.shape[0], PARTS * SLAB, partial.shape[-1])
    received = lax.all_to_all(partial, PREFIX, split_axis=0, concat_axis=0, tiled=True)
    blocks = 2 * y_size
    return add_up(xh, [received], width * blocks, blocks)


def solution(mesh):
    shape = (2, mesh.shape["batch"] // 2, mesh.shape["prefix"] // 4, 2, 2)
    fine = Mesh(mesh.devices.reshape(shape), SUB_AXES)
    batch = ("xh", "y")
    placed = (
        P(batch, None, PREFIX),
        P(PREFIX, None),
        P(PREFIX, None),
        P(batch, None, None),
        P(batch, None, None),
        P(batch),
        P(PREFIX, batch),
    )
    return jax.shard_map(
        on_device,
        mesh=fine,
        in_specs=placed,
        out_specs=P(batch + PREFIX, None),
        check_vma=False,
    )
```

profile of v0, /device:TPU:1, one launch (start us, length us, event | category | flops | bytes accessed | tf_op | source)
XLA Modules:
  0.0 151.2 jit_solution(9157299227718754138)
XLA Ops:
  6.5 1.2 copy-done.2
  11.0 3.3 %collective-permute-start = (bf16[2,160,256]{2,1,0:T(8,128)(2,1)S(1)}, bf16[2,160,256]{2,1,0:T(8,128)(2,1)S(1)}, u32[]{:S(2)}, u32[]{:S(2)}) collective-permute-start(bf16[2,160,256]{2,1,0:T(8,128)(2,1)S(1)} %get-tuple-element.62), channel_id=1, source_target_pairs={{0,1},{1,0},{2,3},{3,2},{4,5},{5,4},{6,7},{7,6},{8,9},{9,8},{10,11... | collective-permute-start | bytes 491528 | tf_op jit(solution)/shard_map/ppermute | solution.py:469
  14.3 6.5 %all-to-all-start = ((bf16[8,2,128,128]{3,2,1,0:T(8,128)(2,1)}), bf16[8,2,128,128]{3,2,1,0:T(8,128)(2,1)S(1)}, u32[]{:S(2)}, u32[]{:S(2)}) async-start(bf16[8,2,128,128]{3,2,1,0:T(8,128)(2,1)} %get-tuple-element.37), calls=%async_computation | async-start | bytes 1048576 | tf_op jit(solution)/shard_map/all_to_all | solution.py:489
  20.9 1.3 collective-permute-start.1
  22.2 2.5 %collective-permute-start.2 = (bf16[160,512]{1,0:T(8,128)(2,1)S(1)}, bf16[160,512]{1,0:T(8,128)(2,1)S(1)}, u32[]{:S(2)}, u32[]{:S(2)}) collective-permute-start(bf16[160,512]{1,0:T(8,128)(2,1)S(1)} %get-tuple-element.60), channel_id=1, source_target_pairs={{0,128},{128,0},{1,129},{129,1},{2,130},{130,2},{3,131},{131,3},{4... | collective-permute-start | bytes 491528 | tf_op jit(solution)/shard_map/ppermute | solution.py:486
  26.4 6.6 %collective-permute-done.2 = bf16[160,512]{1,0:T(8,128)(2,1)S(1)} collective-permute-done((bf16[160,512]{1,0:T(8,128)(2,1)S(1)}, bf16[160,512]{1,0:T(8,128)(2,1)S(1)}, u32[]{:S(2)}, u32[]{:S(2)}) %collective-permute-start.2) | collective-permute-done | bytes 163872 | tf_op jit(solution)/shard_map/ppermute | solution.py:486
  33.1 1.5 collective-permute-done.3
  35.5 5.6 %attend_own.1 = (f32[1024,128]{1,0:T(8,128)S(1)}, f32[1024,128]{1,0:T(8,128)S(1)}) custom-call(s32[1]{0:T(128)} %constant.44.clone.1.held_ref, bf16[1024,128]{1,0:T(8,128)(2,1)S(1)} %bitcast.32, bf16[4,128,128]{2,1,0:T(8,128)(2,1)S(1)} %get-tuple-element.65.refs_1_, bf16[4,128,128]{2,1,0:T(8,128)(2,1)S(1)} %get-tuple-element.64.refs_2_, ...), custom_call_target="tpu_custom_call" | custom-call | flops 5750000128 | bytes 1 | tf_op jit(solution)/shard_map/attend_own/pallas_call | solution.py:253
  41.2 2.7 %collective-permute-start.5 = (bf16[2,896,128]{2,1,0:T(8,128)(2,1)S(1)}, bf16[2,896,128]{2,1,0:T(8,128)(2,1)S(1)}, u32[]{:S(2)}, u32[]{:S(2)}) collective-permute-start(bf16[2,896,128]{2,1,0:T(8,128)(2,1)S(1)} %unpack_heads.1.refs_2_), channel_id=1, source_target_pairs={{0,96},{32,0},{64,32},{96,64},{1,97},{33,1},{65,33},{97,65},{2,98}... | collective-permute-start | bytes 1376264 | tf_op jit(solution)/shard_map/ppermute | solution.py:503
  45.2 10.7 %attend_first.1 = (f32[4096,128]{1,0:T(8,128)S(1)}, f32[4096,128]{1,0:T(8,128)S(1)}) custom-call(s32[1]{0:T(128)} %constant.44.clone.1.held_ref, bf16[4096,128]{1,0:T(8,128)(2,1)S(1)} %bitcast.34, bf16[2,512,128]{2,1,0:T(8,128)(2,1)S(1)} %get-tuple-element.31.refs_3_.refs_1_, bf16[2,896,128]{2,1,0:T(8,128)(2,1)S(1)} %unpack_heads.1.refs_2_, ...), custom_call_target="tpu_custom_call" | custom-call | flops 12650000384 | bytes 1 | tf_op jit(solution)/shard_map/attend_first/pallas_call | solution.py:253
  56.0 2.8 %collective-permute-start.7 = (bf16[896,128]{1,0:T(8,128)(2,1)S(1)}, bf16[896,128]{1,0:T(8,128)(2,1)S(1)}, u32[]{:S(2)}, u32[]{:S(2)}) collective-permute-start(bf16[896,128]{1,0:T(8,128)(2,1)S(1)} %slice_bitcast_fusion), channel_id=1, source_target_pairs={{0,96},{32,0},{64,32},{96,64},{1,97},{33,1},{65,33},{97,65},{2,98}... | collective-permute-start | bytes 688136 | tf_op jit(solution)/shard_map/ppermute | solution.py:517
  59.0 12.5 %attend_more.1 = (f32[4096,128]{1,0:T(8,128)S(1)}, f32[4096,128]{1,0:T(8,128)S(1)}) custom-call(s32[1]{0:T(128)} %constant.44.clone.1.held_ref, bf16[4096,128]{1,0:T(8,128)(2,1)S(1)} %bitcast.35, bf16[2,896,128]{2,1,0:T(8,128)(2,1)S(1)} %collective-permute-done.4.refs_1_, bf16[2,896,128]{2,1,0:T(8,128)(2,1)S(1)} %collective-permute-done.5.refs_2_, ...), custom_call_target="tpu_custom_call" | custom-call | flops 16099999744 | bytes 1 | tf_op jit(solution)/shard_map/attend_more/pallas_call | solution.py:253
  71.9 2.1 %attend_far.2 = bf16[1072,128]{1,0:T(8,128)(2,1)S(1)} custom-call(s32[1]{0:T(128)} %constant.44.clone.1.held_ref, bf16[4096,128]{1,0:T(8,128)(2,1)S(1)} %bitcast.36, f32[4096,128]{1,0:T(8,128)S(1)} %get-tuple-element.42.refs_1_, f32[4096,128]{1,0:T(8,128)S(1)} %get-tuple-element.43.refs_2_, bf16[896,128]{1,0:T(8,128)(2,1)S(1)} %collective-permute-done.6.refs_3_, ...), custom_call_target="tpu_custom_call" | custom-call | flops 2300000000 | bytes 1 | tf_op jit(solution)/shard_map/attend_far/pallas_call | solution.py:253
  74.0 3.1 %collective-permute-start.8 = (bf16[1072,128]{1,0:T(8,128)(2,1)S(1)}, bf16[1072,128]{1,0:T(8,128)(2,1)S(1)}, u32[]{:S(2)}, u32[]{:S(2)}) collective-permute-start(bf16[1072,128]{1,0:T(8,128)(2,1)S(1)} %attend_far.2), channel_id=1, source_target_pairs={{0,1},{1,0},{2,3},{3,2},{4,5},{5,4},{6,7},{7,6},{8,9},{9,8},{10,11... | collective-permute-start | bytes 823304 | tf_op jit(solution)/shard_map/ppermute | solution.py:525
  77.1 2.1 %attend_far.3 = bf16[1072,128]{1,0:T(8,128)(2,1)S(1)} custom-call(s32[1]{0:T(128)} %constant.44.clone.1.held_ref, bf16[4096,128]{1,0:T(8,128)(2,1)S(1)} %bitcast.37, f32[4096,128]{1,0:T(8,128)S(1)} %get-tuple-element.42.refs_1_, f32[4096,128]{1,0:T(8,128)S(1)} %get-tuple-element.43.refs_2_, bf16[896,128]{1,0:T(8,128)(2,1)S(1)} %collective-permute-done.6.refs_3_, ...), custom_call_target="tpu_custom_call" | custom-call | flops 2300000000 | bytes 1 | tf_op jit(solution)/shard_map/attend_far/pallas_call | solution.py:253
  79.3 2.4 %attend_near.2 = (f32[1024,128]{1,0:T(8,128)S(1)}, f32[16,128]{1,0:T(8,128)S(1)}, bf16[1072,128]{1,0:T(8,128)(2,1)S(1)}) custom-call(s32[1]{0:T(128)} %constant.44.clone.1.held_ref, bf16[4096,128]{1,0:T(8,128)(2,1)S(1)} %bitcast.38, f32[4096,128]{1,0:T(8,128)S(1)} %get-tuple-element.42.refs_1_, f32[4096,128]{1,0:T(8,128)S(1)} %get-tuple-element.43.refs_2_, ...), custom_call_target="tpu_custom_call" | custom-call | flops 2300000000 | bytes 1 | tf_op jit(solution)/shard_map/attend_near/pallas_call | solution.py:253
  82.1 2.4 %attend_near.3 = (f32[1024,128]{1,0:T(8,128)S(1)}, f32[16,128]{1,0:T(8,128)S(1)}, bf16[1072,128]{1,0:T(8,128)(2,1)S(1)}) custom-call(s32[1]{0:T(128)} %constant.44.clone.1.held_ref, bf16[4096,128]{1,0:T(8,128)(2,1)S(1)} %bitcast.39, f32[4096,128]{1,0:T(8,128)S(1)} %get-tuple-element.42.refs_1_, f32[4096,128]{1,0:T(8,128)S(1)} %get-tuple-element.43.refs_2_, ...), custom_call_target="tpu_custom_call" | custom-call | flops 2300000000 | bytes 1 | tf_op jit(solution)/shard_map/attend_near/pallas_call | solution.py:253
  84.5 1.5 %collective-permute-start.12 = (bf16[1072,128]{1,0:T(8,128)(2,1)S(1)}, bf16[1072,128]{1,0:T(8,128)(2,1)S(1)}, u32[]{:S(2)}, u32[]{:S(2)}) collective-permute-start(bf16[1072,128]{1,0:T(8,128)(2,1)S(1)} %get-tuple-element.56), channel_id=1, source_target_pairs={{0,2},{2,0},{1,3},{3,1},{4,6},{6,4},{5,7},{7,5},{8,10},{10,8},{9,1... | collective-permute-start | bytes 823304 | tf_op jit(solution)/shard_map/ppermute | solution.py:531
  86.0 3.7 %collective-permute-done.10.refs_3_ = bf16[1072,128]{1,0:T(8,128)(2,1)S(1)} collective-permute-done((bf16[1072,128]{1,0:T(8,128)(2,1)S(1)}, bf16[1072,128]{1,0:T(8,128)(2,1)S(1)}, u32[]{:S(2)}, u32[]{:S(2)}) %collective-permute-start.10) | collective-permute-done | bytes 274464 | tf_op jit(solution)/shard_map/ppermute | solution.py:531
  90.7 4.9 %collective-permute-done.12.refs_3_ = bf16[1072,128]{1,0:T(8,128)(2,1)S(1)} collective-permute-done((bf16[1072,128]{1,0:T(8,128)(2,1)S(1)}, bf16[1072,128]{1,0:T(8,128)(2,1)S(1)}, u32[]{:S(2)}, u32[]{:S(2)}) %collective-permute-start.12) | collective-permute-done | bytes 274464 | tf_op jit(solution)/shard_map/ppermute | solution.py:531
  96.6 1.4 collective-permute-start.13
  99.5 2.9 %project.1 = bf16[32,2,8,1280]{3,2,1,0:T(8,128)(2,1)} custom-call(s32[1]{0:T(128)} %constant.44.clone.1.held_ref, bf16[1280,1024]{1,0:T(8,128)(2,1)S(1)} %copy-done.1, bf16[256,512]{1,0:T(8,128)(2,1)S(1)} %merge_last.2.refs_1_, bf16[256,512]{1,0:T(8,128)(2,1)S(1)} %collective-permute-done.11.refs_2_, bf16[256,512]{1,0:T(8,128)(2,1)S(1)} %merge_last.3.refs_3_, ...), custom_call_target="tpu_custom_call" | custom-call | flops 3449999872 | bytes 1 | tf_op jit(solution)/shard_map/project/pallas_call | solution.py:253
  102.5 7.3 %all-to-all-start.1 = ((bf16[32,16,1280]{2,1,0:T(8,128)(2,1)}), bf16[32,16,1280]{2,1,0:T(8,128)(2,1)S(1)}, u32[]{:S(2)}, u32[]{:S(2)}) async-start(bf16[32,16,1280]{2,1,0:T(8,128)(2,1)} %bitcast.21), calls=%async_computation.1 | async-start | bytes 2621440 | tf_op jit(solution)/shard_map/all_to_all | solution.py:544
  109.8 33.7 %all-to-all-done.1.refs_1_ = bf16[32,16,1280]{2,1,0:T(8,128)(2,1)S(1)} async-done(((bf16[32,16,1280]{2,1,0:T(8,128)(2,1)}), bf16[32,16,1280]{2,1,0:T(8,128)(2,1)S(1)}, u32[]{:S(2)}, u32[]{:S(2)}) %all-to-all-start.1) | async-done | bytes 1310752 | tf_op jit(solution)/shard_map/all_to_all | solution.py:544
  (51 shorter events, 12.9 us)
Async XLA Ops:
  6.5 37.4 %all-gather.5.cloned.1.call-start = ((), (), s32[]{:S(2)}) async-start(), calls=%async_computation.3 | async-start | bytes 1310720 | tf_op jit(solution)/shard_map/all_gather | solution.py:493
  6.5 1.2 copy-start.2
  7.8 1.2 copy-start.3
  9.0 1.8 %copy-start.5 = (bf16[256,640]{1,0:T(8,128)(2,1)S(1)}, bf16[256,640]{1,0:T(8,128)(2,1)}, u32[]{:S(2)}) copy-start(bf16[256,640]{1,0:T(8,128)(2,1)} %param.13) | copy-start | bytes 983044
  11.0 9.8 %collective-permute-start = (bf16[2,160,256]{2,1,0:T(8,128)(2,1)S(1)}, bf16[2,160,256]{2,1,0:T(8,128)(2,1)S(1)}, u32[]{:S(2)}, u32[]{:S(2)}) collective-permute-start(bf16[2,160,256]{2,1,0:T(8,128)(2,1)S(1)} %get-tuple-element.62), channel_id=1, source_target_pairs={{0,1},{1,0},{2,3},{3,2},{4,5},{5,4},{6,7},{7,6},{8,9},{9,8},{10,11... | collective-permute-start | bytes 491528 | tf_op jit(solution)/shard_map/ppermute | solution.py:469
  14.3 26.9 %all-to-all-start = ((bf16[8,2,128,128]{3,2,1,0:T(8,128)(2,1)}), bf16[8,2,128,128]{3,2,1,0:T(8,128)(2,1)S(1)}, u32[]{:S(2)}, u32[]{:S(2)}) async-start(bf16[8,2,128,128]{3,2,1,0:T(8,128)(2,1)} %get-tuple-element.37), calls=%async_computation | async-start | bytes 1048576 | tf_op jit(solution)/shard_map/all_to_all | solution.py:489
  20.8 65.3 %all-gather.3.cloned.1.call-start = ((), (), s32[]{:S(2)}) async-start(), calls=%async_computation.2 | async-start | bytes 3276800 | tf_op jit(solution)/shard_map/all_gather | solution.py:506
  20.9 14.7 %copy-start = (bf16[32,2,8,2,128]{4,2,0,3,1:T(8,128)(2,1)S(1)}, bf16[32,2,8,2,128]{4,2,0,3,1:T(8,128)(2,1)}, u32[]{:S(2)}) copy-start(bf16[32,2,8,2,128]{4,2,0,3,1:T(8,128)(2,1)} %copy.14) | copy-start | bytes 786436
  20.9 5.6 %collective-permute-start.1 = (bf16[160,512]{1,0:T(8,128)(2,1)S(1)}, bf16[160,512]{1,0:T(8,128)(2,1)S(1)}, u32[]{:S(2)}, u32[]{:S(2)}) collective-permute-start(bf16[160,512]{1,0:T(8,128)(2,1)S(1)} %get-tuple-element.61), channel_id=1, source_target_pairs={{0,2},{2,0},{1,3},{3,1},{4,6},{6,4},{5,7},{7,5},{8,10},{10,8},{9,1... | collective-permute-start | bytes 491528 | tf_op jit(solution)/shard_map/ppermute | solution.py:485
  22.2 10.9 %collective-permute-start.2 = (bf16[160,512]{1,0:T(8,128)(2,1)S(1)}, bf16[160,512]{1,0:T(8,128)(2,1)S(1)}, u32[]{:S(2)}, u32[]{:S(2)}) collective-permute-start(bf16[160,512]{1,0:T(8,128)(2,1)S(1)} %get-tuple-element.60), channel_id=1, source_target_pairs={{0,128},{128,0},{1,129},{129,1},{2,130},{130,2},{3,131},{131,3},{4... | collective-permute-start | bytes 491528 | tf_op jit(solution)/shard_map/ppermute | solution.py:486
  24.6 9.9 %collective-permute-start.3 = (bf16[160,512]{1,0:T(8,128)(2,1)S(1)}, bf16[160,512]{1,0:T(8,128)(2,1)S(1)}, u32[]{:S(2)}, u32[]{:S(2)}) collective-permute-start(bf16[160,512]{1,0:T(8,128)(2,1)S(1)} %get-tuple-element.61), channel_id=1, source_target_pairs={{0,130},{2,128},{128,2},{130,0},{1,131},{3,129},{129,3},{131,1},{4... | collective-permute-start | bytes 491528 | tf_op jit(solution)/shard_map/ppermute | solution.py:487
  41.2 14.7 %collective-permute-start.5 = (bf16[2,896,128]{2,1,0:T(8,128)(2,1)S(1)}, bf16[2,896,128]{2,1,0:T(8,128)(2,1)S(1)}, u32[]{:S(2)}, u32[]{:S(2)}) collective-permute-start(bf16[2,896,128]{2,1,0:T(8,128)(2,1)S(1)} %unpack_heads.1.refs_2_), channel_id=1, source_target_pairs={{0,96},{32,0},{64,32},{96,64},{1,97},{33,1},{65,33},{97,65},{2,98}... | collective-permute-start | bytes 1376264 | tf_op jit(solution)/shard_map/ppermute | solution.py:503
  43.9 14.8 %collective-permute-start.4 = (bf16[2,896,128]{2,1,0:T(8,128)(2,1)S(1)}, bf16[2,896,128]{2,1,0:T(8,128)(2,1)S(1)}, u32[]{:S(2)}, u32[]{:S(2)}) collective-permute-start(bf16[2,896,128]{2,1,0:T(8,128)(2,1)S(1)} %unpack_heads.1.refs_2_), channel_id=1, source_target_pairs={{0,32},{32,64},{64,96},{96,0},{1,33},{33,65},{65,97},{97,1},{2,34}... | collective-permute-start | bytes 1376264 | tf_op jit(solution)/shard_map/ppermute | solution.py:502
  56.0 15.6 %collective-permute-start.7 = (bf16[896,128]{1,0:T(8,128)(2,1)S(1)}, bf16[896,128]{1,0:T(8,128)(2,1)S(1)}, u32[]{:S(2)}, u32[]{:S(2)}) collective-permute-start(bf16[896,128]{1,0:T(8,128)(2,1)S(1)} %slice_bitcast_fusion), channel_id=1, source_target_pairs={{0,96},{32,0},{64,32},{96,64},{1,97},{33,1},{65,33},{97,65},{2,98}... | collective-permute-start | bytes 688136 | tf_op jit(solution)/shard_map/ppermute | solution.py:517
  58.7 13.1 %collective-permute-start.6 = (bf16[896,128]{1,0:T(8,128)(2,1)S(1)}, bf16[896,128]{1,0:T(8,128)(2,1)S(1)}, u32[]{:S(2)}, u32[]{:S(2)}) collective-permute-start(bf16[896,128]{1,0:T(8,128)(2,1)S(1)} %slice_bitcast_fusion.1), channel_id=1, source_target_pairs={{0,32},{32,64},{64,96},{96,0},{1,33},{33,65},{65,97},{97,1},{2,34}... | collective-permute-start | bytes 688136 | tf_op jit(solution)/shard_map/ppermute | solution.py:516
  74.0 5.3 %collective-permute-start.8 = (bf16[1072,128]{1,0:T(8,128)(2,1)S(1)}, bf16[1072,128]{1,0:T(8,128)(2,1)S(1)}, u32[]{:S(2)}, u32[]{:S(2)}) collective-permute-start(bf16[1072,128]{1,0:T(8,128)(2,1)S(1)} %attend_far.2), channel_id=1, source_target_pairs={{0,1},{1,0},{2,3},{3,2},{4,5},{5,4},{6,7},{7,6},{8,9},{9,8},{10,11... | collective-permute-start | bytes 823304 | tf_op jit(solution)/shard_map/ppermute | solution.py:525
  79.2 2.9 %collective-permute-start.9 = (bf16[1072,128]{1,0:T(8,128)(2,1)S(1)}, bf16[1072,128]{1,0:T(8,128)(2,1)S(1)}, u32[]{:S(2)}, u32[]{:S(2)}) collective-permute-start(bf16[1072,128]{1,0:T(8,128)(2,1)S(1)} %attend_far.3), channel_id=1, source_target_pairs={{0,1},{1,0},{2,3},{3,2},{4,5},{5,4},{6,7},{7,6},{8,9},{9,8},{10,11... | collective-permute-start | bytes 823304 | tf_op jit(solution)/shard_map/ppermute | solution.py:525
  81.7 8.0 %copy-start.4 = (s32[4]{0:T(128)S(1)}, s32[4]{0:T(128)}, u32[]{:S(2)}) copy-start(s32[4]{0:T(128)} %refs_0_.3) | copy-start | bytes 52
  81.7 8.0 %collective-permute-start.10 = (bf16[1072,128]{1,0:T(8,128)(2,1)S(1)}, bf16[1072,128]{1,0:T(8,128)(2,1)S(1)}, u32[]{:S(2)}, u32[]{:S(2)}) collective-permute-start(bf16[1072,128]{1,0:T(8,128)(2,1)S(1)} %get-tuple-element.53), channel_id=1, source_target_pairs={{0,2},{2,0},{1,3},{3,1},{4,6},{6,4},{5,7},{7,5},{8,10},{10,8},{9,1... | collective-permute-start | bytes 823304 | tf_op jit(solution)/shard_map/ppermute | solution.py:531
  84.5 11.1 %collective-permute-start.12 = (bf16[1072,128]{1,0:T(8,128)(2,1)S(1)}, bf16[1072,128]{1,0:T(8,128)(2,1)S(1)}, u32[]{:S(2)}, u32[]{:S(2)}) collective-permute-start(bf16[1072,128]{1,0:T(8,128)(2,1)S(1)} %get-tuple-element.56), channel_id=1, source_target_pairs={{0,2},{2,0},{1,3},{3,1},{4,6},{6,4},{5,7},{7,5},{8,10},{10,8},{9,1... | collective-permute-start | bytes 823304 | tf_op jit(solution)/shard_map/ppermute | solution.py:531
  95.6 4.0 %copy-start.1 = (bf16[1280,1024]{1,0:T(8,128)(2,1)S(1)}, bf16[1280,1024]{1,0:T(8,128)(2,1)}, u32[]{:S(2)}) copy-start(bf16[1280,1024]{1,0:T(8,128)(2,1)} %all-gather.3.cloned.1.call-done.refs_0_) | copy-start | bytes 7864324
  96.6 2.6 %collective-permute-start.13 = (bf16[256,512]{1,0:T(8,128)(2,1)S(1)}, bf16[256,512]{1,0:T(8,128)(2,1)S(1)}, u32[]{:S(2)}, u32[]{:S(2)}) collective-permute-start(bf16[256,512]{1,0:T(8,128)(2,1)S(1)} %merge_last.3.refs_3_), channel_id=1, source_target_pairs={{0,1},{1,0},{2,3},{3,2},{4,5},{5,4},{6,7},{7,6},{8,9},{9,8},{10,11... | collective-permute-start | bytes 786440 | tf_op jit(solution)/shard_map/ppermute | solution.py:541
  98.0 1.5 %collective-permute-start.11 = (bf16[256,512]{1,0:T(8,128)(2,1)S(1)}, bf16[256,512]{1,0:T(8,128)(2,1)S(1)}, u32[]{:S(2)}, u32[]{:S(2)}) collective-permute-start(bf16[256,512]{1,0:T(8,128)(2,1)S(1)} %merge_last.2.refs_1_), channel_id=1, source_target_pairs={{0,1},{1,0},{2,3},{3,2},{4,5},{5,4},{6,7},{7,6},{8,9},{9,8},{10,11... | collective-permute-start | bytes 786440 | tf_op jit(solution)/shard_map/ppermute | solution.py:541
  102.5 41.0 %all-to-all-start.1 = ((bf16[32,16,1280]{2,1,0:T(8,128)(2,1)}), bf16[32,16,1280]{2,1,0:T(8,128)(2,1)S(1)}, u32[]{:S(2)}, u32[]{:S(2)}) async-start(bf16[32,16,1280]{2,1,0:T(8,128)(2,1)} %bitcast.21), calls=%async_computation.1 | async-start | bytes 2621440 | tf_op jit(solution)/shard_map/all_to_all | solution.py:544
  (1 other events, 1.0 us)
Sparse Core Ops, SparseCore 0:
  10.9 28.8 all-gather.4
  41.6 43.3 all-gather.2
where the time goes:
time: 152 us; the launch traced here: 151 us
  waiting for transfers between devices  52.9 us (35%)
  Pallas kernels  44.6 us (29%)
  starting transfers between devices  33.4 us (22%)
  between operations  13.6 us (9%)
  local copies, waits for them, and re-layouts  5.62 us (4%)
    pallas_call x13, Pallas kernels, run(): pl.pallas_call(lambda held_ref, *refs: kernel(*refs), name=name, in_specs...  44.6 us
    all_to_all x1, waiting for transfers between devices, on_device(): lax.all_to_all(partial, PREFIX, split_axis=0, concat_axis=0, tiled=True)  33.7 us
    ppermute x2, waiting for transfers between devices, on_device(): near_x.append(lax.ppermute(sent, 'xl', SWAP))  8.54 us
    all_to_all x1, starting transfers between devices, on_device(): lax.all_to_all(partial, PREFIX, split_axis=0, concat_axis=0, tiled=True)  7.33 us
    ppermute x1, waiting for transfers between devices, on_device(): w_h = lax.ppermute(w_own, 'xh', SWAP)  6.63 us
    all_to_all x1, starting transfers between devices, on_device(): lax.all_to_all(after(sent, both), 'z', split_axis=0, concat_axis=0, tiled...  6.45 us
    ppermute x1, starting transfers between devices, weight_of_core(): return jnp.concatenate([of_c, lax.ppermute(sent, 'c', SWAP)], axis=2)  3.33 us
    ppermute x2, starting transfers between devices, on_device(): far_c = [lax.ppermute(f, 'c', SWAP) for f in far]  3.24 us
  transfers between devices with their start and end apart: 18, of which 9 were waited for; matrix products, arithmetic and copies ran while one was open for 2% of the time, Pallas kernels for 26%

commit v1 on v0

--- a/solution.py
+++ b/solution.py
@@ -63,12 +63,31 @@
     return top, total, acc_in[...]
 
 
+def rows_of(pieces):
+    parts = [ref[at:to, :] for ref, at, to in pieces]
+    return parts[0] if len(parts) == 1 else jnp.concatenate(parts, axis=0)
+
+
+def absorb_blocks(state, q, blocks, chunk=CHUNK):
+    sizes = [keys.shape[0] for keys, _ in blocks]
+    ends = [sum(sizes[: i + 1]) for i in range(len(sizes))]
+    at = 0
+    while at < ends[-1]:
+        to = min(at + chunk, ends[-1])
+        spans = []
+        for (keys, values), end, size in zip(blocks, ends, sizes):
+            low, high = max(at, end - size), min(to, end)
+            if low < high:
+                spans.append((keys, values, low - end + size, high - end + size))
+        keys = rows_of([(k, low, high) for k, _, low, high in spans])
+        values = rows_of([(v, low, high) for _, v, low, high in spans])
+        state = absorb(state, score_dot(q, keys), values)
+        at = to
+    return state
+
+
 def absorb_block(state, q, keys, values, chunk=CHUNK):
-    count = keys.shape[0]
-    for at in range(0, count, chunk):
-        to = min(at + chunk, count)
-        state = absorb(state, score_dot(q, keys[at:to, :]), values[at:to, :])
-    return state
+    return absorb_blocks(state, q, [(keys, values)], chunk)
 
 
 def first_own_kernel(q_ref, rk_ref, rv_ref, block, acc_out, stat_out):
@@ -119,8 +138,8 @@
 def middle_kernel(count, q_ref, *refs):
     blocks, (acc_in, stat_in, acc_out, stat_out) = refs[:count], refs[count:]
     state = load_state(acc_in, stat_in)
-    for block in blocks:
-        state = absorb_block(state, q_ref[...], block.at[0], block.at[1])
+    pairs = [(block.at[0], block.at[1]) for block in blocks]
+    state = absorb_blocks(state, q_ref[...], pairs)
     store_state(state, acc_out, stat_out)
 
 
@@ -443,13 +462,14 @@
         out_ref[1, i * count : (i + 1) * count] = got_ref[source, 1]
 
 
-def unpack(z, got):
+def unpack(z, got, order):
     groups, two, count, width = got.shape
     out = jax.ShapeDtypeStruct((two, (groups - 1) * count, width), BF16)
     return call(
         unpack_kernel,
         "unpack_heads",
         1,
+        order,
         grid=(1,),
         in_specs=[SMEM, whole(got)],
         out_specs=whole(out),
@@ -497,8 +517,8 @@
     head = z * HEAD_SIZE
     rk = lax.dynamic_slice_in_dim(resp_keys, head, HEAD_SIZE, 2)
     rv = lax.dynamic_slice_in_dim(resp_values, head, HEAD_SIZE, 2)
-    state = first_own(q_own, rk, rv, own_block, (w_x, w_h, w_xh))
-    near_y = unpack(z, after(got, state[0]))
+    state = first_own(q_own, rk, rv, own_block, ())
+    near_y = unpack(z, after(got, state[0]), (w_x, w_h, w_xh))
     from_below = lax.ppermute(near_y, "y", up)
     from_above = lax.ppermute(near_y, "y", down)
     here = jnp.concatenate([w_own, w_x], axis=1)

time: 152 us -> 148 us (0.974)
  Pallas kernels: 44.6 us -> 42.9 us
    ppermute x1, waiting for transfers between devices: 6.63 us -> 3.6 us  [on_device(): w_h = lax.ppermute(w_own, 'xh', SWAP)]
    ppermute x2, waiting for transfers between devices: 8.54 us -> 5.53 us  [on_device(): near_x.append(lax.ppermute(sent, 'xl', SWAP))]
    all_gather x1, waiting for transfers between devices: 0.01 us -> 3.01 us  [on_device(): lax.all_gather(jnp.concatenate([here, there], axis=0), 'y', axis=0, tiled...]
    all_to_all x1, waiting for transfers between devices: 0.01 us -> 2.97 us  [on_device(): lax.all_to_all(after(sent, both), 'z', split_axis=0, concat_axis=0, tiled...]
    ppermute x1, starting transfers between devices: 2.45 us -> 0.64 us  [on_device(): w_h = lax.ppermute(w_own, 'xh', SWAP)]
    pallas_call x13, Pallas kernels: 44.6 us -> 42.9 us  [run(): pl.pallas_call(lambda held_ref, *refs: kernel(*refs), name=name, in_specs...]
    ppermute x1, starting transfers between devices: 0.2 us -> 1.82 us  [on_device(): w_xh = lax.ppermute(w_sent, ('xh', 'xl'), [(i, 3 - i) for i in range(4)])]
    ppermute x1, waiting for transfers between devices: 0.36 us -> 1.95 us  [on_device(): far_k = lax.ppermute(after(from_below, state[0])[0], 'y', up)]
  transfers between devices with their start and end apart: 18 -> 18, of which waited for: 9 -> 9; matrix products, arithmetic and copies ran while one was open for 2% -> 2% of each run, Pallas kernels for 26% -> 25%
where the time goes in v1:
time: 148 us
  waiting for transfers between devices  52.3 us (35%)
  Pallas kernels  42.9 us (29%)
  starting transfers between devices  32.4 us (22%)
  between operations  13.6 us (9%)
  local copies, waits for them, and re-layouts  5.63 us (4%)
    pallas_call x13, Pallas kernels, run(): pl.pallas_call(lambda held_ref, *refs: kernel(*refs), name=name, in_specs...  42.9 us
    all_to_all x1, waiting for transfers between devices, on_device(): lax.all_to_all(partial, PREFIX, split_axis=0, concat_axis=0, tiled=True)  33.7 us
    all_to_all x1, starting transfers between devices, on_device(): lax.all_to_all(partial, PREFIX, split_axis=0, concat_axis=0, tiled=True)  7.13 us
    all_to_all x1, starting transfers between devices, on_device(): lax.all_to_all(after(sent, both), 'z', split_axis=0, concat_axis=0, tiled...  6.45 us
    ppermute x2, waiting for transfers between devices, on_device(): near_x.append(lax.ppermute(sent, 'xl', SWAP))  5.53 us
    ppermute x1, waiting for transfers between devices, on_device(): w_h = lax.ppermute(w_own, 'xh', SWAP)  3.6 us
    ppermute x1, starting transfers between devices, weight_of_core(): return jnp.concatenate([of_c, lax.ppermute(sent, 'c', SWAP)], axis=2)  3.33 us
    all_gather x1, waiting for transfers between devices, on_device(): lax.all_gather(jnp.concatenate([here, there], axis=0), 'y', axis=0, tiled...  3.01 us
  transfers between devices with their start and end apart: 18, of which 9 were waited for; matrix products, arithmetic and copies ran while one was open for 2% of the time, Pallas kernels for 25%

profile of v1, /device:TPU:1, one launch (start us, length us, event | category | flops | bytes accessed | tf_op | source)
XLA Modules:
  0.0 148.0 jit_solution(7209859385886351469)
XLA Ops:
  11.0 3.3 %collective-permute-start = (bf16[2,160,256]{2,1,0:T(8,128)(2,1)S(1)}, bf16[2,160,256]{2,1,0:T(8,128)(2,1)S(1)}, u32[]{:S(2)}, u32[]{:S(2)}) collective-permute-start(bf16[2,160,256]{2,1,0:T(8,128)(2,1)S(1)} %get-tuple-element.62), channel_id=1, source_target_pairs={{0,1},{1,0},{2,3},{3,2},{4,5},{5,4},{6,7},{7,6},{8,9},{9,8},{10,11... | collective-permute-start | bytes 491528 | tf_op jit(solution)/shard_map/ppermute | solution.py:489
  14.3 6.5 %all-to-all-start = ((bf16[8,2,128,128]{3,2,1,0:T(8,128)(2,1)}), bf16[8,2,128,128]{3,2,1,0:T(8,128)(2,1)S(1)}, u32[]{:S(2)}, u32[]{:S(2)}) async-start(bf16[8,2,128,128]{3,2,1,0:T(8,128)(2,1)} %get-tuple-element.37), calls=%async_computation | async-start | bytes 1048576 | tf_op jit(solution)/shard_map/all_to_all | solution.py:509
  21.9 1.3 collective-permute-start.1
  23.2 1.8 %collective-permute-start.3 = (bf16[160,512]{1,0:T(8,128)(2,1)S(1)}, bf16[160,512]{1,0:T(8,128)(2,1)S(1)}, u32[]{:S(2)}, u32[]{:S(2)}) collective-permute-start(bf16[160,512]{1,0:T(8,128)(2,1)S(1)} %get-tuple-element.61), channel_id=1, source_target_pairs={{0,130},{2,128},{128,2},{130,0},{1,131},{3,129},{129,3},{131,1},{4... | collective-permute-start | bytes 491528 | tf_op jit(solution)/shard_map/ppermute | solution.py:507
  25.6 5.6 %attend_own.1 = (f32[1024,128]{1,0:T(8,128)S(1)}, f32[1024,128]{1,0:T(8,128)S(1)}) custom-call(s32[1]{0:T(128)} %constant.44.clone.1.held_ref, bf16[1024,128]{1,0:T(8,128)(2,1)S(1)} %bitcast.32, bf16[4,128,128]{2,1,0:T(8,128)(2,1)S(1)} %get-tuple-element.65.refs_1_, bf16[4,128,128]{2,1,0:T(8,128)(2,1)S(1)} %get-tuple-element.64.refs_2_, ...), custom_call_target="tpu_custom_call" | custom-call | flops 5750000128 | bytes 1 | tf_op jit(solution)/shard_map/attend_own/pallas_call | solution.py:272
  31.3 3.6 %collective-permute-done.2 = bf16[160,512]{1,0:T(8,128)(2,1)S(1)} collective-permute-done((bf16[160,512]{1,0:T(8,128)(2,1)S(1)}, bf16[160,512]{1,0:T(8,128)(2,1)S(1)}, u32[]{:S(2)}, u32[]{:S(2)}) %collective-permute-start.2) | collective-permute-done | bytes 163872 | tf_op jit(solution)/shard_map/ppermute | solution.py:506
  35.8 3.0 %all-to-all-done.refs_1_ = bf16[8,2,128,128]{3,2,1,0:T(8,128)(2,1)S(1)} async-done(((bf16[8,2,128,128]{3,2,1,0:T(8,128)(2,1)}), bf16[8,2,128,128]{3,2,1,0:T(8,128)(2,1)S(1)}, u32[]{:S(2)}, u32[]{:S(2)}) %all-to-all-start) | async-done | bytes 524320 | tf_op jit(solution)/shard_map/all_to_all | solution.py:509
  38.8 2.8 %collective-permute-start.5 = (bf16[2,896,128]{2,1,0:T(8,128)(2,1)S(1)}, bf16[2,896,128]{2,1,0:T(8,128)(2,1)S(1)}, u32[]{:S(2)}, u32[]{:S(2)}) collective-permute-start(bf16[2,896,128]{2,1,0:T(8,128)(2,1)S(1)} %unpack_heads.1.refs_2_), channel_id=1, source_target_pairs={{0,96},{32,0},{64,32},{96,64},{1,97},{33,1},{65,33},{97,65},{2,98}... | collective-permute-start | bytes 1376264 | tf_op jit(solution)/shard_map/ppermute | solution.py:523
  43.0 10.7 %attend_first.1 = (f32[4096,128]{1,0:T(8,128)S(1)}, f32[4096,128]{1,0:T(8,128)S(1)}) custom-call(s32[1]{0:T(128)} %constant.44.clone.1.held_ref, bf16[4096,128]{1,0:T(8,128)(2,1)S(1)} %bitcast.34, bf16[2,512,128]{2,1,0:T(8,128)(2,1)S(1)} %get-tuple-element.31.refs_3_.refs_1_, bf16[2,896,128]{2,1,0:T(8,128)(2,1)S(1)} %unpack_heads.1.refs_2_, ...), custom_call_target="tpu_custom_call" | custom-call | flops 12650000384 | bytes 1 | tf_op jit(solution)/shard_map/attend_first/pallas_call | solution.py:272
  53.7 2.8 %collective-permute-start.7 = (bf16[896,128]{1,0:T(8,128)(2,1)S(1)}, bf16[896,128]{1,0:T(8,128)(2,1)S(1)}, u32[]{:S(2)}, u32[]{:S(2)}) collective-permute-start(bf16[896,128]{1,0:T(8,128)(2,1)S(1)} %slice_bitcast_fusion), channel_id=1, source_target_pairs={{0,96},{32,0},{64,32},{96,64},{1,97},{33,1},{65,33},{97,65},{2,98}... | collective-permute-start | bytes 688136 | tf_op jit(solution)/shard_map/ppermute | solution.py:537
  56.7 10.8 %attend_more.1 = (f32[4096,128]{1,0:T(8,128)S(1)}, f32[4096,128]{1,0:T(8,128)S(1)}) custom-call(s32[1]{0:T(128)} %constant.44.clone.1.held_ref, bf16[4096,128]{1,0:T(8,128)(2,1)S(1)} %bitcast.35, bf16[2,896,128]{2,1,0:T(8,128)(2,1)S(1)} %collective-permute-done.4.refs_1_, bf16[2,896,128]{2,1,0:T(8,128)(2,1)S(1)} %collective-permute-done.5.refs_2_, ...), custom_call_target="tpu_custom_call" | custom-call | flops 16099999744 | bytes 1 | tf_op jit(solution)/shard_map/attend_more/pallas_call | solution.py:272
  67.6 1.9 %collective-permute-done.6.refs_3_ = bf16[896,128]{1,0:T(8,128)(2,1)S(1)} collective-permute-done((bf16[896,128]{1,0:T(8,128)(2,1)S(1)}, bf16[896,128]{1,0:T(8,128)(2,1)S(1)}, u32[]{:S(2)}, u32[]{:S(2)}) %collective-permute-start.6) | collective-permute-done | bytes 229408 | tf_op jit(solution)/shard_map/ppermute | solution.py:536
  69.5 2.1 %attend_far.2 = bf16[1072,128]{1,0:T(8,128)(2,1)S(1)} custom-call(s32[1]{0:T(128)} %constant.44.clone.1.held_ref, bf16[4096,128]{1,0:T(8,128)(2,1)S(1)} %bitcast.36, f32[4096,128]{1,0:T(8,128)S(1)} %get-tuple-element.42.refs_1_, f32[4096,128]{1,0:T(8,128)S(1)} %get-tuple-element.43.refs_2_, bf16[896,128]{1,0:T(8,128)(2,1)S(1)} %collective-permute-done.6.refs_3_, ...), custom_call_target="tpu_custom_call" | custom-call | flops 2300000000 | bytes 1 | tf_op jit(solution)/shard_map/attend_far/pallas_call | solution.py:272
  71.6 2.5 %collective-permute-start.8 = (bf16[1072,128]{1,0:T(8,128)(2,1)S(1)}, bf16[1072,128]{1,0:T(8,128)(2,1)S(1)}, u32[]{:S(2)}, u32[]{:S(2)}) collective-permute-start(bf16[1072,128]{1,0:T(8,128)(2,1)S(1)} %attend_far.2), channel_id=1, source_target_pairs={{0,1},{1,0},{2,3},{3,2},{4,5},{5,4},{6,7},{7,6},{8,9},{9,8},{10,11... | collective-permute-start | bytes 823304 | tf_op jit(solution)/shard_map/ppermute | solution.py:545
  74.0 2.1 %attend_far.3 = bf16[1072,128]{1,0:T(8,128)(2,1)S(1)} custom-call(s32[1]{0:T(128)} %constant.44.clone.1.held_ref, bf16[4096,128]{1,0:T(8,128)(2,1)S(1)} %bitcast.37, f32[4096,128]{1,0:T(8,128)S(1)} %get-tuple-element.42.refs_1_, f32[4096,128]{1,0:T(8,128)S(1)} %get-tuple-element.43.refs_2_, bf16[896,128]{1,0:T(8,128)(2,1)S(1)} %collective-permute-done.6.refs_3_, ...), custom_call_target="tpu_custom_call" | custom-call | flops 2300000000 | bytes 1 | tf_op jit(solution)/shard_map/attend_far/pallas_call | solution.py:272
  76.2 2.4 %attend_near.2 = (f32[1024,128]{1,0:T(8,128)S(1)}, f32[16,128]{1,0:T(8,128)S(1)}, bf16[1072,128]{1,0:T(8,128)(2,1)S(1)}) custom-call(s32[1]{0:T(128)} %constant.44.clone.1.held_ref, bf16[4096,128]{1,0:T(8,128)(2,1)S(1)} %bitcast.38, f32[4096,128]{1,0:T(8,128)S(1)} %get-tuple-element.42.refs_1_, f32[4096,128]{1,0:T(8,128)S(1)} %get-tuple-element.43.refs_2_, ...), custom_call_target="tpu_custom_call" | custom-call | flops 2300000000 | bytes 1 | tf_op jit(solution)/shard_map/attend_near/pallas_call | solution.py:272
  78.7 1.5 %collective-permute-start.10 = (bf16[1072,128]{1,0:T(8,128)(2,1)S(1)}, bf16[1072,128]{1,0:T(8,128)(2,1)S(1)}, u32[]{:S(2)}, u32[]{:S(2)}) collective-permute-start(bf16[1072,128]{1,0:T(8,128)(2,1)S(1)} %get-tuple-element.53), channel_id=1, source_target_pairs={{0,2},{2,0},{1,3},{3,1},{4,6},{6,4},{5,7},{7,5},{8,10},{10,8},{9,1... | collective-permute-start | bytes 823304 | tf_op jit(solution)/shard_map/ppermute | solution.py:551
  80.2 2.5 %attend_near.3 = (f32[1024,128]{1,0:T(8,128)S(1)}, f32[16,128]{1,0:T(8,128)S(1)}, bf16[1072,128]{1,0:T(8,128)(2,1)S(1)}) custom-call(s32[1]{0:T(128)} %constant.44.clone.1.held_ref, bf16[4096,128]{1,0:T(8,128)(2,1)S(1)} %bitcast.39, f32[4096,128]{1,0:T(8,128)S(1)} %get-tuple-element.42.refs_1_, f32[4096,128]{1,0:T(8,128)S(1)} %get-tuple-element.43.refs_2_, ...), custom_call_target="tpu_custom_call" | custom-call | flops 2300000000 | bytes 1 | tf_op jit(solution)/shard_map/attend_near/pallas_call | solution.py:272
  82.9 3.0 %all-gather.3.cloned.1.call-done.refs_0_ = bf16[1280,1024]{1,0:T(8,128)(2,1)} async-done(((bf16[320,1024]{1,0:T(8,128)(2,1)}), bf16[1280,1024]{1,0:T(8,128)(2,1)}) %all-gather.3.cloned.1.call-update) | async-done | bytes 2621456 | tf_op jit(solution)/shard_map/all_gather | solution.py:526
  87.6 4.9 %collective-permute-done.12.refs_3_ = bf16[1072,128]{1,0:T(8,128)(2,1)S(1)} collective-permute-done((bf16[1072,128]{1,0:T(8,128)(2,1)S(1)}, bf16[1072,128]{1,0:T(8,128)(2,1)S(1)}, u32[]{:S(2)}, u32[]{:S(2)}) %collective-permute-start.12) | collective-permute-done | bytes 274464 | tf_op jit(solution)/shard_map/ppermute | solution.py:551
  93.5 1.4 collective-permute-start.13
  96.5 2.9 %project.1 = bf16[32,2,8,1280]{3,2,1,0:T(8,128)(2,1)} custom-call(s32[1]{0:T(128)} %constant.44.clone.1.held_ref, bf16[1280,1024]{1,0:T(8,128)(2,1)S(1)} %copy-done.1, bf16[256,512]{1,0:T(8,128)(2,1)S(1)} %merge_last.2.refs_1_, bf16[256,512]{1,0:T(8,128)(2,1)S(1)} %collective-permute-done.11.refs_2_, bf16[256,512]{1,0:T(8,128)(2,1)S(1)} %merge_last.3.refs_3_, ...), custom_call_target="tpu_custom_call" | custom-call | flops 3449999872 | bytes 1 | tf_op jit(solution)/shard_map/project/pallas_call | solution.py:272
  99.4 7.1 %all-to-all-start.1 = ((bf16[32,16,1280]{2,1,0:T(8,128)(2,1)}), bf16[32,16,1280]{2,1,0:T(8,128)(2,1)S(1)}, u32[]{:S(2)}, u32[]{:S(2)}) async-start(bf16[32,16,1280]{2,1,0:T(8,128)(2,1)} %bitcast.21), calls=%async_computation.1 | async-start | bytes 2621440 | tf_op jit(solution)/shard_map/all_to_all | solution.py:564
  106.5 33.7 %all-to-all-done.1.refs_1_ = bf16[32,16,1280]{2,1,0:T(8,128)(2,1)S(1)} async-done(((bf16[32,16,1280]{2,1,0:T(8,128)(2,1)}), bf16[32,16,1280]{2,1,0:T(8,128)(2,1)S(1)}, u32[]{:S(2)}, u32[]{:S(2)}) %all-to-all-start.1) | async-done | bytes 1310752 | tf_op jit(solution)/shard_map/all_to_all | solution.py:564
  (51 shorter events, 14.2 us)
Async XLA Ops:
  6.5 35.1 %all-gather.5.cloned.1.call-start = ((), (), s32[]{:S(2)}) async-start(), calls=%async_computation.3 | async-start | bytes 1310720 | tf_op jit(solution)/shard_map/all_gather | solution.py:513
  6.5 1.2 copy-start.2
  7.8 1.2 copy-start.3
  9.0 1.8 %copy-start.5 = (bf16[256,640]{1,0:T(8,128)(2,1)S(1)}, bf16[256,640]{1,0:T(8,128)(2,1)}, u32[]{:S(2)}) copy-start(bf16[256,640]{1,0:T(8,128)(2,1)} %param.13) | copy-start | bytes 983044
  10.9 14.7 %copy-start = (bf16[32,2,8,2,128]{4,2,0,3,1:T(8,128)(2,1)S(1)}, bf16[32,2,8,2,128]{4,2,0,3,1:T(8,128)(2,1)}, u32[]{:S(2)}) copy-start(bf16[32,2,8,2,128]{4,2,0,3,1:T(8,128)(2,1)} %copy.14) | copy-start | bytes 786436
  11.0 10.8 %collective-permute-start = (bf16[2,160,256]{2,1,0:T(8,128)(2,1)S(1)}, bf16[2,160,256]{2,1,0:T(8,128)(2,1)S(1)}, u32[]{:S(2)}, u32[]{:S(2)}) collective-permute-start(bf16[2,160,256]{2,1,0:T(8,128)(2,1)S(1)} %get-tuple-element.62), channel_id=1, source_target_pairs={{0,1},{1,0},{2,3},{3,2},{4,5},{5,4},{6,7},{7,6},{8,9},{9,8},{10,11... | collective-permute-start | bytes 491528 | tf_op jit(solution)/shard_map/ppermute | solution.py:489
  14.3 24.5 %all-to-all-start = ((bf16[8,2,128,128]{3,2,1,0:T(8,128)(2,1)}), bf16[8,2,128,128]{3,2,1,0:T(8,128)(2,1)S(1)}, u32[]{:S(2)}, u32[]{:S(2)}) async-start(bf16[8,2,128,128]{3,2,1,0:T(8,128)(2,1)} %get-tuple-element.37), calls=%async_computation | async-start | bytes 1048576 | tf_op jit(solution)/shard_map/all_to_all | solution.py:509
  20.8 65.2 %all-gather.3.cloned.1.call-start = ((), (), s32[]{:S(2)}) async-start(), calls=%async_computation.2 | async-start | bytes 3276800 | tf_op jit(solution)/shard_map/all_gather | solution.py:526
  21.9 9.4 %collective-permute-start.1 = (bf16[160,512]{1,0:T(8,128)(2,1)S(1)}, bf16[160,512]{1,0:T(8,128)(2,1)S(1)}, u32[]{:S(2)}, u32[]{:S(2)}) collective-permute-start(bf16[160,512]{1,0:T(8,128)(2,1)S(1)} %get-tuple-element.61), channel_id=1, source_target_pairs={{0,2},{2,0},{1,3},{3,1},{4,6},{6,4},{5,7},{7,5},{8,10},{10,8},{9,1... | collective-permute-start | bytes 491528 | tf_op jit(solution)/shard_map/ppermute | solution.py:505
  23.2 11.7 %collective-permute-start.3 = (bf16[160,512]{1,0:T(8,128)(2,1)S(1)}, bf16[160,512]{1,0:T(8,128)(2,1)S(1)}, u32[]{:S(2)}, u32[]{:S(2)}) collective-permute-start(bf16[160,512]{1,0:T(8,128)(2,1)S(1)} %get-tuple-element.61), channel_id=1, source_target_pairs={{0,130},{2,128},{128,2},{130,0},{1,131},{3,129},{129,3},{131,1},{4... | collective-permute-start | bytes 491528 | tf_op jit(solution)/shard_map/ppermute | solution.py:507
  25.0 9.9 %collective-permute-start.2 = (bf16[160,512]{1,0:T(8,128)(2,1)S(1)}, bf16[160,512]{1,0:T(8,128)(2,1)S(1)}, u32[]{:S(2)}, u32[]{:S(2)}) collective-permute-start(bf16[160,512]{1,0:T(8,128)(2,1)S(1)} %get-tuple-element.60), channel_id=1, source_target_pairs={{0,128},{128,0},{1,129},{129,1},{2,130},{130,2},{3,131},{131,3},{4... | collective-permute-start | bytes 491528 | tf_op jit(solution)/shard_map/ppermute | solution.py:506
  38.8 14.8 %collective-permute-start.5 = (bf16[2,896,128]{2,1,0:T(8,128)(2,1)S(1)}, bf16[2,896,128]{2,1,0:T(8,128)(2,1)S(1)}, u32[]{:S(2)}, u32[]{:S(2)}) collective-permute-start(bf16[2,896,128]{2,1,0:T(8,128)(2,1)S(1)} %unpack_heads.1.refs_2_), channel_id=1, source_target_pairs={{0,96},{32,0},{64,32},{96,64},{1,97},{33,1},{65,33},{97,65},{2,98}... | collective-permute-start | bytes 1376264 | tf_op jit(solution)/shard_map/ppermute | solution.py:523
  41.6 14.8 %collective-permute-start.4 = (bf16[2,896,128]{2,1,0:T(8,128)(2,1)S(1)}, bf16[2,896,128]{2,1,0:T(8,128)(2,1)S(1)}, u32[]{:S(2)}, u32[]{:S(2)}) collective-permute-start(bf16[2,896,128]{2,1,0:T(8,128)(2,1)S(1)} %unpack_heads.1.refs_2_), channel_id=1, source_target_pairs={{0,32},{32,64},{64,96},{96,0},{1,33},{33,65},{65,97},{97,1},{2,34}... | collective-permute-start | bytes 1376264 | tf_op jit(solution)/shard_map/ppermute | solution.py:522
  53.7 13.9 %collective-permute-start.7 = (bf16[896,128]{1,0:T(8,128)(2,1)S(1)}, bf16[896,128]{1,0:T(8,128)(2,1)S(1)}, u32[]{:S(2)}, u32[]{:S(2)}) collective-permute-start(bf16[896,128]{1,0:T(8,128)(2,1)S(1)} %slice_bitcast_fusion), channel_id=1, source_target_pairs={{0,96},{32,0},{64,32},{96,64},{1,97},{33,1},{65,33},{97,65},{2,98}... | collective-permute-start | bytes 688136 | tf_op jit(solution)/shard_map/ppermute | solution.py:537
  56.5 13.0 %collective-permute-start.6 = (bf16[896,128]{1,0:T(8,128)(2,1)S(1)}, bf16[896,128]{1,0:T(8,128)(2,1)S(1)}, u32[]{:S(2)}, u32[]{:S(2)}) collective-permute-start(bf16[896,128]{1,0:T(8,128)(2,1)S(1)} %slice_bitcast_fusion.1), channel_id=1, source_target_pairs={{0,32},{32,64},{64,96},{96,0},{1,33},{33,65},{65,97},{97,1},{2,34}... | collective-permute-start | bytes 688136 | tf_op jit(solution)/shard_map/ppermute | solution.py:536
  71.6 4.6 %collective-permute-start.8 = (bf16[1072,128]{1,0:T(8,128)(2,1)S(1)}, bf16[1072,128]{1,0:T(8,128)(2,1)S(1)}, u32[]{:S(2)}, u32[]{:S(2)}) collective-permute-start(bf16[1072,128]{1,0:T(8,128)(2,1)S(1)} %attend_far.2), channel_id=1, source_target_pairs={{0,1},{1,0},{2,3},{3,2},{4,5},{5,4},{6,7},{7,6},{8,9},{9,8},{10,11... | collective-permute-start | bytes 823304 | tf_op jit(solution)/shard_map/ppermute | solution.py:545
  76.1 4.1 %collective-permute-start.9 = (bf16[1072,128]{1,0:T(8,128)(2,1)S(1)}, bf16[1072,128]{1,0:T(8,128)(2,1)S(1)}, u32[]{:S(2)}, u32[]{:S(2)}) collective-permute-start(bf16[1072,128]{1,0:T(8,128)(2,1)S(1)} %attend_far.3), channel_id=1, source_target_pairs={{0,1},{1,0},{2,3},{3,2},{4,5},{5,4},{6,7},{7,6},{8,9},{9,8},{10,11... | collective-permute-start | bytes 823304 | tf_op jit(solution)/shard_map/ppermute | solution.py:545
  78.7 8.0 %copy-start.4 = (s32[4]{0:T(128)S(1)}, s32[4]{0:T(128)}, u32[]{:S(2)}) copy-start(s32[4]{0:T(128)} %refs_0_.3) | copy-start | bytes 52
  78.7 8.0 %collective-permute-start.10 = (bf16[1072,128]{1,0:T(8,128)(2,1)S(1)}, bf16[1072,128]{1,0:T(8,128)(2,1)S(1)}, u32[]{:S(2)}, u32[]{:S(2)}) collective-permute-start(bf16[1072,128]{1,0:T(8,128)(2,1)S(1)} %get-tuple-element.53), channel_id=1, source_target_pairs={{0,2},{2,0},{1,3},{3,1},{4,6},{6,4},{5,7},{7,5},{8,10},{10,8},{9,1... | collective-permute-start | bytes 823304 | tf_op jit(solution)/shard_map/ppermute | solution.py:551
  82.6 9.9 %collective-permute-start.12 = (bf16[1072,128]{1,0:T(8,128)(2,1)S(1)}, bf16[1072,128]{1,0:T(8,128)(2,1)S(1)}, u32[]{:S(2)}, u32[]{:S(2)}) collective-permute-start(bf16[1072,128]{1,0:T(8,128)(2,1)S(1)} %get-tuple-element.56), channel_id=1, source_target_pairs={{0,2},{2,0},{1,3},{3,1},{4,6},{6,4},{5,7},{7,5},{8,10},{10,8},{9,1... | collective-permute-start | bytes 823304 | tf_op jit(solution)/shard_map/ppermute | solution.py:551
  92.5 4.0 %copy-start.1 = (bf16[1280,1024]{1,0:T(8,128)(2,1)S(1)}, bf16[1280,1024]{1,0:T(8,128)(2,1)}, u32[]{:S(2)}) copy-start(bf16[1280,1024]{1,0:T(8,128)(2,1)} %all-gather.3.cloned.1.call-done.refs_0_) | copy-start | bytes 7864324
  93.5 2.6 %collective-permute-start.13 = (bf16[256,512]{1,0:T(8,128)(2,1)S(1)}, bf16[256,512]{1,0:T(8,128)(2,1)S(1)}, u32[]{:S(2)}, u32[]{:S(2)}) collective-permute-start(bf16[256,512]{1,0:T(8,128)(2,1)S(1)} %merge_last.3.refs_3_), channel_id=1, source_target_pairs={{0,1},{1,0},{2,3},{3,2},{4,5},{5,4},{6,7},{7,6},{8,9},{9,8},{10,11... | collective-permute-start | bytes 786440 | tf_op jit(solution)/shard_map/ppermute | solution.py:561
  94.9 1.5 %collective-permute-start.11 = (bf16[256,512]{1,0:T(8,128)(2,1)S(1)}, bf16[256,512]{1,0:T(8,128)(2,1)S(1)}, u32[]{:S(2)}, u32[]{:S(2)}) collective-permute-start(bf16[256,512]{1,0:T(8,128)(2,1)S(1)} %merge_last.2.refs_1_), channel_id=1, source_target_pairs={{0,1},{1,0},{2,3},{3,2},{4,5},{5,4},{6,7},{7,6},{8,9},{9,8},{10,11... | collective-permute-start | bytes 786440 | tf_op jit(solution)/shard_map/ppermute | solution.py:561
  99.4 40.8 %all-to-all-start.1 = ((bf16[32,16,1280]{2,1,0:T(8,128)(2,1)}), bf16[32,16,1280]{2,1,0:T(8,128)(2,1)S(1)}, u32[]{:S(2)}, u32[]{:S(2)}) async-start(bf16[32,16,1280]{2,1,0:T(8,128)(2,1)} %bitcast.21), calls=%async_computation.1 | async-start | bytes 2621440 | tf_op jit(solution)/shard_map/all_to_all | solution.py:564
  (1 other events, 1.0 us)
Sparse Core Ops, SparseCore 0:
  10.9 29.8 all-gather.4
  42.6 43.3 all-gather.2

commit v2 on v1

--- a/solution.py
+++ b/solution.py
@@ -84,6 +84,16 @@
         state = absorb(state, score_dot(q, keys), values)
         at = to
     return state
+
+
+def first_rows(block):
+    cut = block.shape[1] // CHUNK * CHUNK
+    return block.at[0, :cut, :], block.at[1, :cut, :]
+
+
+def other_rows(block):
+    cut = block.shape[1] // CHUNK * CHUNK
+    return block.at[0, cut:, :], block.at[1, cut:, :]
 
 
 def absorb_block(state, q, keys, values, chunk=CHUNK):
@@ -131,14 +141,15 @@
         absorb_first(0)
 
     state = load_state(acc_out, stat_out)
-    state = absorb_block(state, q_ref[...], near_block.at[0], near_block.at[1])
+    state = absorb_blocks(state, q_ref[...], [first_rows(near_block)])
     store_state(state, acc_out, stat_out)
 
 
 def middle_kernel(count, q_ref, *refs):
     blocks, (acc_in, stat_in, acc_out, stat_out) = refs[:count], refs[count:]
     state = load_state(acc_in, stat_in)
-    pairs = [(block.at[0], block.at[1]) for block in blocks]
+    near, below, above = blocks
+    pairs = [other_rows(near), (below.at[0], below.at[1]), first_rows(above)]
     state = absorb_blocks(state, q_ref[...], pairs)
     store_state(state, acc_out, stat_out)
 
@@ -187,8 +198,9 @@
 
 def finish(q_ref, blocks, acc_in, stat_in):
     state = load_state(acc_in, stat_in)
-    keys, values = blocks
-    top, total, acc = absorb_block(state, q_ref[...], keys, values)
+    above, keys, values = blocks
+    pairs = [other_rows(above), (keys, values)]
+    top, total, acc = absorb_blocks(state, q_ref[...], pairs)
     return acc / total, top + jnp.log2(total)
 
 
@@ -535,9 +547,9 @@
     state = first_all(q_all, own_block, near_y, state, 1024, ())
     far_k = lax.ppermute(after(from_below, state[0])[0], "y", up)
     far_v = lax.ppermute(after(from_above, state[0])[1], "y", down)
-    state = attend_more(q_all, [from_below, from_above], state, 1024, ())
+    state = attend_more(q_all, [near_y, from_below, from_above], state, 1024, ())
     half = 2 * slot_rows
-    blocks = [far_k, far_v]
+    blocks = [from_above, far_k, far_v]
     far = []
     for part in range(PARTS):
         order = (far[-1],) if far else ()

time: 148 us -> 147 us (level)
  waiting for transfers between devices: 52.3 us -> 50.6 us
  transfers between devices with their start and end apart: 18 -> 18, of which waited for: 9 -> 9; matrix products, arithmetic and copies ran while one was open for 2% -> 2% of each run, Pallas kernels for 25% -> 26%
where the time goes in v2:
time: 147 us
  waiting for transfers between devices  50.6 us (34%)
  Pallas kernels  43.4 us (30%)
  starting transfers between devices  32.2 us (22%)
  between operations  13.6 us (9%)
  local copies, waits for them, and re-layouts  5.63 us (4%)
    pallas_call x13, Pallas kernels, run(): pl.pallas_call(lambda held_ref, *refs: kernel(*refs), name=name, in_specs...  43.4 us
    all_to_all x1, waiting for transfers between devices, on_device(): lax.all_to_all(partial, PREFIX, split_axis=0, concat_axis=0, tiled=True)  33.7 us
    all_to_all x1, starting transfers between devices, on_device(): lax.all_to_all(after(sent, both), 'z', split_axis=0, concat_axis=0, tiled...  6.45 us
    all_to_all x1, starting transfers between devices, on_device(): lax.all_to_all(partial, PREFIX, split_axis=0, concat_axis=0, tiled=True)  6.36 us
    ppermute x2, waiting for transfers between devices, on_device(): near_x.append(lax.ppermute(sent, 'xl', SWAP))  5.41 us
    ppermute x1, waiting for transfers between devices, on_device(): w_h = lax.ppermute(w_own, 'xh', SWAP)  3.6 us
    ppermute x1, starting transfers between devices, weight_of_core(): return jnp.concatenate([of_c, lax.ppermute(sent, 'c', SWAP)], axis=2)  3.33 us
    ppermute x2, starting transfers between devices, on_device(): far_c = [lax.ppermute(f, 'c', SWAP) for f in far]  3.12 us
  transfers between devices with their start and end apart: 18, of which 9 were waited for; matrix products, arithmetic and copies ran while one was open for 2% of the time, Pallas kernels for 26%

profile of v2, /device:TPU:1, one launch (start us, length us, event | category | flops | bytes accessed | tf_op | source)
XLA Modules:
  0.0 146.6 jit_solution(14340985484858214719)
XLA Ops:
  6.5 1.2 copy-done.2
  11.0 3.3 %collective-permute-start = (bf16[2,160,256]{2,1,0:T(8,128)(2,1)S(1)}, bf16[2,160,256]{2,1,0:T(8,128)(2,1)S(1)}, u32[]{:S(2)}, u32[]{:S(2)}) collective-permute-start(bf16[2,160,256]{2,1,0:T(8,128)(2,1)S(1)} %get-tuple-element.62), channel_id=1, source_target_pairs={{0,1},{1,0},{2,3},{3,2},{4,5},{5,4},{6,7},{7,6},{8,9},{9,8},{10,11... | collective-permute-start | bytes 491528 | tf_op jit(solution)/shard_map/ppermute | solution.py:501
  14.3 6.5 %all-to-all-start = ((bf16[8,2,128,128]{3,2,1,0:T(8,128)(2,1)}), bf16[8,2,128,128]{3,2,1,0:T(8,128)(2,1)S(1)}, u32[]{:S(2)}, u32[]{:S(2)}) async-start(bf16[8,2,128,128]{3,2,1,0:T(8,128)(2,1)} %get-tuple-element.37), calls=%async_computation | async-start | bytes 1048576 | tf_op jit(solution)/shard_map/all_to_all | solution.py:521
  21.9 1.3 collective-permute-start.1
  23.2 1.8 %collective-permute-start.3 = (bf16[160,512]{1,0:T(8,128)(2,1)S(1)}, bf16[160,512]{1,0:T(8,128)(2,1)S(1)}, u32[]{:S(2)}, u32[]{:S(2)}) collective-permute-start(bf16[160,512]{1,0:T(8,128)(2,1)S(1)} %get-tuple-element.61), channel_id=1, source_target_pairs={{0,130},{2,128},{128,2},{130,0},{1,131},{3,129},{129,3},{131,1},{4... | collective-permute-start | bytes 491528 | tf_op jit(solution)/shard_map/ppermute | solution.py:519
  25.6 5.6 %attend_own.1 = (f32[1024,128]{1,0:T(8,128)S(1)}, f32[1024,128]{1,0:T(8,128)S(1)}) custom-call(s32[1]{0:T(128)} %constant.44.clone.1.held_ref, bf16[1024,128]{1,0:T(8,128)(2,1)S(1)} %bitcast.32, bf16[4,128,128]{2,1,0:T(8,128)(2,1)S(1)} %get-tuple-element.65.refs_1_, bf16[4,128,128]{2,1,0:T(8,128)(2,1)S(1)} %get-tuple-element.64.refs_2_, ...), custom_call_target="tpu_custom_call" | custom-call | flops 5750000128 | bytes 1 | tf_op jit(solution)/shard_map/attend_own/pallas_call | solution.py:284
  31.3 3.6 %collective-permute-done.2 = bf16[160,512]{1,0:T(8,128)(2,1)S(1)} collective-permute-done((bf16[160,512]{1,0:T(8,128)(2,1)S(1)}, bf16[160,512]{1,0:T(8,128)(2,1)S(1)}, u32[]{:S(2)}, u32[]{:S(2)}) %collective-permute-start.2) | collective-permute-done | bytes 163872 | tf_op jit(solution)/shard_map/ppermute | solution.py:518
  35.8 3.0 %all-to-all-done.refs_1_ = bf16[8,2,128,128]{3,2,1,0:T(8,128)(2,1)S(1)} async-done(((bf16[8,2,128,128]{3,2,1,0:T(8,128)(2,1)}), bf16[8,2,128,128]{3,2,1,0:T(8,128)(2,1)S(1)}, u32[]{:S(2)}, u32[]{:S(2)}) %all-to-all-start) | async-done | bytes 524320 | tf_op jit(solution)/shard_map/all_to_all | solution.py:521
  38.8 2.8 %collective-permute-start.5 = (bf16[2,896,128]{2,1,0:T(8,128)(2,1)S(1)}, bf16[2,896,128]{2,1,0:T(8,128)(2,1)S(1)}, u32[]{:S(2)}, u32[]{:S(2)}) collective-permute-start(bf16[2,896,128]{2,1,0:T(8,128)(2,1)S(1)} %unpack_heads.1.refs_2_.refs_1_), channel_id=1, source_target_pairs={{0,96},{32,0},{64,32},{96,64},{1,97},{33,1},{65,33},{97,65},{2,98}... | collective-permute-start | bytes 1376264 | tf_op jit(solution)/shard_map/ppermute | solution.py:535
  43.0 9.2 %attend_first.1 = (f32[4096,128]{1,0:T(8,128)S(1)}, f32[4096,128]{1,0:T(8,128)S(1)}) custom-call(s32[1]{0:T(128)} %constant.44.clone.1.held_ref, bf16[4096,128]{1,0:T(8,128)(2,1)S(1)} %bitcast.34, bf16[2,512,128]{2,1,0:T(8,128)(2,1)S(1)} %get-tuple-element.31.refs_3_.refs_1_, bf16[2,896,128]{2,1,0:T(8,128)(2,1)S(1)} %unpack_heads.1.refs_2_.refs_1_, ...), custom_call_target="tpu_custom_call" | custom-call | flops 12650000384 | bytes 1 | tf_op jit(solution)/shard_map/attend_first/pallas_call | solution.py:284
  52.2 2.8 %collective-permute-start.7 = (bf16[896,128]{1,0:T(8,128)(2,1)S(1)}, bf16[896,128]{1,0:T(8,128)(2,1)S(1)}, u32[]{:S(2)}, u32[]{:S(2)}) collective-permute-start(bf16[896,128]{1,0:T(8,128)(2,1)S(1)} %slice_bitcast_fusion), channel_id=1, source_target_pairs={{0,96},{32,0},{64,32},{96,64},{1,97},{33,1},{65,33},{97,65},{2,98}... | collective-permute-start | bytes 688136 | tf_op jit(solution)/shard_map/ppermute | solution.py:549
  55.2 10.8 %attend_more.1 = (f32[4096,128]{1,0:T(8,128)S(1)}, f32[4096,128]{1,0:T(8,128)S(1)}) custom-call(s32[1]{0:T(128)} %constant.44.clone.1.held_ref, bf16[4096,128]{1,0:T(8,128)(2,1)S(1)} %bitcast.35, bf16[2,896,128]{2,1,0:T(8,128)(2,1)S(1)} %unpack_heads.1.refs_2_.refs_1_, bf16[2,896,128]{2,1,0:T(8,128)(2,1)S(1)} %collective-permute-done.4.refs_2_, ...), custom_call_target="tpu_custom_call" | custom-call | flops 24149999616 | bytes 1 | tf_op jit(solution)/shard_map/attend_more/pallas_call | solution.py:284
  66.9 2.5 %attend_far.2 = bf16[1072,128]{1,0:T(8,128)(2,1)S(1)} custom-call(s32[1]{0:T(128)} %constant.44.clone.1.held_ref, bf16[4096,128]{1,0:T(8,128)(2,1)S(1)} %bitcast.36, f32[4096,128]{1,0:T(8,128)S(1)} %get-tuple-element.42.refs_1_, f32[4096,128]{1,0:T(8,128)S(1)} %get-tuple-element.43.refs_2_, bf16[2,896,128]{2,1,0:T(8,128)(2,1)S(1)} %collective-permute-done.5.refs_3_, ...), custom_call_target="tpu_custom_call" | custom-call | flops 2300000000 | bytes 1 | tf_op jit(solution)/shard_map/attend_far/pallas_call | solution.py:284
  69.4 3.0 %collective-permute-start.8 = (bf16[1072,128]{1,0:T(8,128)(2,1)S(1)}, bf16[1072,128]{1,0:T(8,128)(2,1)S(1)}, u32[]{:S(2)}, u32[]{:S(2)}) collective-permute-start(bf16[1072,128]{1,0:T(8,128)(2,1)S(1)} %attend_far.2), channel_id=1, source_target_pairs={{0,1},{1,0},{2,3},{3,2},{4,5},{5,4},{6,7},{7,6},{8,9},{9,8},{10,11... | collective-permute-start | bytes 823304 | tf_op jit(solution)/shard_map/ppermute | solution.py:557
  72.4 2.5 %attend_far.3 = bf16[1072,128]{1,0:T(8,128)(2,1)S(1)} custom-call(s32[1]{0:T(128)} %constant.44.clone.1.held_ref, bf16[4096,128]{1,0:T(8,128)(2,1)S(1)} %bitcast.37, f32[4096,128]{1,0:T(8,128)S(1)} %get-tuple-element.42.refs_1_, f32[4096,128]{1,0:T(8,128)S(1)} %get-tuple-element.43.refs_2_, bf16[2,896,128]{2,1,0:T(8,128)(2,1)S(1)} %collective-permute-done.5.refs_3_, ...), custom_call_target="tpu_custom_call" | custom-call | flops 2300000000 | bytes 1 | tf_op jit(solution)/shard_map/attend_far/pallas_call | solution.py:284
  75.1 3.0 %attend_near.2 = (f32[1024,128]{1,0:T(8,128)S(1)}, f32[16,128]{1,0:T(8,128)S(1)}, bf16[1072,128]{1,0:T(8,128)(2,1)S(1)}) custom-call(s32[1]{0:T(128)} %constant.44.clone.1.held_ref, bf16[4096,128]{1,0:T(8,128)(2,1)S(1)} %bitcast.38, f32[4096,128]{1,0:T(8,128)S(1)} %get-tuple-element.42.refs_1_, f32[4096,128]{1,0:T(8,128)S(1)} %get-tuple-element.43.refs_2_, ...), custom_call_target="tpu_custom_call" | custom-call | flops 2300000000 | bytes 1 | tf_op jit(solution)/shard_map/attend_near/pallas_call | solution.py:284
  78.0 1.5 %collective-permute-start.10 = (bf16[1072,128]{1,0:T(8,128)(2,1)S(1)}, bf16[1072,128]{1,0:T(8,128)(2,1)S(1)}, u32[]{:S(2)}, u32[]{:S(2)}) collective-permute-start(bf16[1072,128]{1,0:T(8,128)(2,1)S(1)} %get-tuple-element.53), channel_id=1, source_target_pairs={{0,2},{2,0},{1,3},{3,1},{4,6},{6,4},{5,7},{7,5},{8,10},{10,8},{9,1... | collective-permute-start | bytes 823304 | tf_op jit(solution)/shard_map/ppermute | solution.py:563
  79.6 2.9 %attend_near.3 = (f32[1024,128]{1,0:T(8,128)S(1)}, f32[16,128]{1,0:T(8,128)S(1)}, bf16[1072,128]{1,0:T(8,128)(2,1)S(1)}) custom-call(s32[1]{0:T(128)} %constant.44.clone.1.held_ref, bf16[4096,128]{1,0:T(8,128)(2,1)S(1)} %bitcast.39, f32[4096,128]{1,0:T(8,128)S(1)} %get-tuple-element.42.refs_1_, f32[4096,128]{1,0:T(8,128)S(1)} %get-tuple-element.43.refs_2_, ...), custom_call_target="tpu_custom_call" | custom-call | flops 2300000000 | bytes 1 | tf_op jit(solution)/shard_map/attend_near/pallas_call | solution.py:284
  82.8 2.6 %all-gather.3.cloned.1.call-done.refs_0_ = bf16[1280,1024]{1,0:T(8,128)(2,1)} async-done(((bf16[320,1024]{1,0:T(8,128)(2,1)}), bf16[1280,1024]{1,0:T(8,128)(2,1)}) %all-gather.3.cloned.1.call-update) | async-done | bytes 2621456 | tf_op jit(solution)/shard_map/all_gather | solution.py:538
  87.0 4.9 %collective-permute-done.12.refs_3_ = bf16[1072,128]{1,0:T(8,128)(2,1)S(1)} collective-permute-done((bf16[1072,128]{1,0:T(8,128)(2,1)S(1)}, bf16[1072,128]{1,0:T(8,128)(2,1)S(1)}, u32[]{:S(2)}, u32[]{:S(2)}) %collective-permute-start.12) | collective-permute-done | bytes 274464 | tf_op jit(solution)/shard_map/ppermute | solution.py:563
  92.9 1.4 collective-permute-start.13
  95.8 2.9 %project.1 = bf16[32,2,8,1280]{3,2,1,0:T(8,128)(2,1)} custom-call(s32[1]{0:T(128)} %constant.44.clone.1.held_ref, bf16[1280,1024]{1,0:T(8,128)(2,1)S(1)} %copy-done.1, bf16[256,512]{1,0:T(8,128)(2,1)S(1)} %merge_last.2.refs_1_, bf16[256,512]{1,0:T(8,128)(2,1)S(1)} %collective-permute-done.11.refs_2_, bf16[256,512]{1,0:T(8,128)(2,1)S(1)} %merge_last.3.refs_3_, ...), custom_call_target="tpu_custom_call" | custom-call | flops 3449999872 | bytes 1 | tf_op jit(solution)/shard_map/project/pallas_call | solution.py:284
  98.8 6.4 %all-to-all-start.1 = ((bf16[32,16,1280]{2,1,0:T(8,128)(2,1)}), bf16[32,16,1280]{2,1,0:T(8,128)(2,1)S(1)}, u32[]{:S(2)}, u32[]{:S(2)}) async-start(bf16[32,16,1280]{2,1,0:T(8,128)(2,1)} %bitcast.21), calls=%async_computation.1 | async-start | bytes 2621440 | tf_op jit(solution)/shard_map/all_to_all | solution.py:576
  105.1 33.7 %all-to-all-done.1.refs_1_ = bf16[32,16,1280]{2,1,0:T(8,128)(2,1)S(1)} async-done(((bf16[32,16,1280]{2,1,0:T(8,128)(2,1)}), bf16[32,16,1280]{2,1,0:T(8,128)(2,1)S(1)}, u32[]{:S(2)}, u32[]{:S(2)}) %all-to-all-start.1) | async-done | bytes 1310752 | tf_op jit(solution)/shard_map/all_to_all | solution.py:576
  (51 shorter events, 13.7 us)
Async XLA Ops:
  6.5 35.1 %all-gather.5.cloned.1.call-start = ((), (), s32[]{:S(2)}) async-start(), calls=%async_computation.3 | async-start | bytes 1310720 | tf_op jit(solution)/shard_map/all_gather | solution.py:525
  6.5 1.2 copy-start.2
  7.8 1.2 copy-start.3
  9.0 1.8 %copy-start.5 = (bf16[256,640]{1,0:T(8,128)(2,1)S(1)}, bf16[256,640]{1,0:T(8,128)(2,1)}, u32[]{:S(2)}) copy-start(bf16[256,640]{1,0:T(8,128)(2,1)} %param.13) | copy-start | bytes 983044
  10.9 14.7 %copy-start = (bf16[32,2,8,2,128]{4,2,0,3,1:T(8,128)(2,1)S(1)}, bf16[32,2,8,2,128]{4,2,0,3,1:T(8,128)(2,1)}, u32[]{:S(2)}) copy-start(bf16[32,2,8,2,128]{4,2,0,3,1:T(8,128)(2,1)} %copy.14) | copy-start | bytes 786436
  11.0 10.8 %collective-permute-start = (bf16[2,160,256]{2,1,0:T(8,128)(2,1)S(1)}, bf16[2,160,256]{2,1,0:T(8,128)(2,1)S(1)}, u32[]{:S(2)}, u32[]{:S(2)}) collective-permute-start(bf16[2,160,256]{2,1,0:T(8,128)(2,1)S(1)} %get-tuple-element.62), channel_id=1, source_target_pairs={{0,1},{1,0},{2,3},{3,2},{4,5},{5,4},{6,7},{7,6},{8,9},{9,8},{10,11... | collective-permute-start | bytes 491528 | tf_op jit(solution)/shard_map/ppermute | solution.py:501
  14.3 24.5 %all-to-all-start = ((bf16[8,2,128,128]{3,2,1,0:T(8,128)(2,1)}), bf16[8,2,128,128]{3,2,1,0:T(8,128)(2,1)S(1)}, u32[]{:S(2)}, u32[]{:S(2)}) async-start(bf16[8,2,128,128]{3,2,1,0:T(8,128)(2,1)} %get-tuple-element.37), calls=%async_computation | async-start | bytes 1048576 | tf_op jit(solution)/shard_map/all_to_all | solution.py:521
  20.8 64.7 %all-gather.3.cloned.1.call-start = ((), (), s32[]{:S(2)}) async-start(), calls=%async_computation.2 | async-start | bytes 3276800 | tf_op jit(solution)/shard_map/all_gather | solution.py:538
  21.9 9.4 %collective-permute-start.1 = (bf16[160,512]{1,0:T(8,128)(2,1)S(1)}, bf16[160,512]{1,0:T(8,128)(2,1)S(1)}, u32[]{:S(2)}, u32[]{:S(2)}) collective-permute-start(bf16[160,512]{1,0:T(8,128)(2,1)S(1)} %get-tuple-element.61), channel_id=1, source_target_pairs={{0,2},{2,0},{1,3},{3,1},{4,6},{6,4},{5,7},{7,5},{8,10},{10,8},{9,1... | collective-permute-start | bytes 491528 | tf_op jit(solution)/shard_map/ppermute | solution.py:517
  23.2 11.7 %collective-permute-start.3 = (bf16[160,512]{1,0:T(8,128)(2,1)S(1)}, bf16[160,512]{1,0:T(8,128)(2,1)S(1)}, u32[]{:S(2)}, u32[]{:S(2)}) collective-permute-start(bf16[160,512]{1,0:T(8,128)(2,1)S(1)} %get-tuple-element.61), channel_id=1, source_target_pairs={{0,130},{2,128},{128,2},{130,0},{1,131},{3,129},{129,3},{131,1},{4... | collective-permute-start | bytes 491528 | tf_op jit(solution)/shard_map/ppermute | solution.py:519
  25.0 9.9 %collective-permute-start.2 = (bf16[160,512]{1,0:T(8,128)(2,1)S(1)}, bf16[160,512]{1,0:T(8,128)(2,1)S(1)}, u32[]{:S(2)}, u32[]{:S(2)}) collective-permute-start(bf16[160,512]{1,0:T(8,128)(2,1)S(1)} %get-tuple-element.60), channel_id=1, source_target_pairs={{0,128},{128,0},{1,129},{129,1},{2,130},{130,2},{3,131},{131,3},{4... | collective-permute-start | bytes 491528 | tf_op jit(solution)/shard_map/ppermute | solution.py:518
  38.8 13.3 %collective-permute-start.5 = (bf16[2,896,128]{2,1,0:T(8,128)(2,1)S(1)}, bf16[2,896,128]{2,1,0:T(8,128)(2,1)S(1)}, u32[]{:S(2)}, u32[]{:S(2)}) collective-permute-start(bf16[2,896,128]{2,1,0:T(8,128)(2,1)S(1)} %unpack_heads.1.refs_2_.refs_1_), channel_id=1, source_target_pairs={{0,96},{32,0},{64,32},{96,64},{1,97},{33,1},{65,33},{97,65},{2,98}... | collective-permute-start | bytes 1376264 | tf_op jit(solution)/shard_map/ppermute | solution.py:535
  41.6 13.3 %collective-permute-start.4 = (bf16[2,896,128]{2,1,0:T(8,128)(2,1)S(1)}, bf16[2,896,128]{2,1,0:T(8,128)(2,1)S(1)}, u32[]{:S(2)}, u32[]{:S(2)}) collective-permute-start(bf16[2,896,128]{2,1,0:T(8,128)(2,1)S(1)} %unpack_heads.1.refs_2_.refs_1_), channel_id=1, source_target_pairs={{0,32},{32,64},{64,96},{96,0},{1,33},{33,65},{65,97},{97,1},{2,34}... | collective-permute-start | bytes 1376264 | tf_op jit(solution)/shard_map/ppermute | solution.py:534
  52.2 13.9 %collective-permute-start.7 = (bf16[896,128]{1,0:T(8,128)(2,1)S(1)}, bf16[896,128]{1,0:T(8,128)(2,1)S(1)}, u32[]{:S(2)}, u32[]{:S(2)}) collective-permute-start(bf16[896,128]{1,0:T(8,128)(2,1)S(1)} %slice_bitcast_fusion), channel_id=1, source_target_pairs={{0,96},{32,0},{64,32},{96,64},{1,97},{33,1},{65,33},{97,65},{2,98}... | collective-permute-start | bytes 688136 | tf_op jit(solution)/shard_map/ppermute | solution.py:549
  55.0 11.9 %collective-permute-start.6 = (bf16[896,128]{1,0:T(8,128)(2,1)S(1)}, bf16[896,128]{1,0:T(8,128)(2,1)S(1)}, u32[]{:S(2)}, u32[]{:S(2)}) collective-permute-start(bf16[896,128]{1,0:T(8,128)(2,1)S(1)} %slice_bitcast_fusion.1), channel_id=1, source_target_pairs={{0,32},{32,64},{64,96},{96,0},{1,33},{33,65},{65,97},{97,1},{2,34}... | collective-permute-start | bytes 688136 | tf_op jit(solution)/shard_map/ppermute | solution.py:548
  69.4 5.7 %collective-permute-start.8 = (bf16[1072,128]{1,0:T(8,128)(2,1)S(1)}, bf16[1072,128]{1,0:T(8,128)(2,1)S(1)}, u32[]{:S(2)}, u32[]{:S(2)}) collective-permute-start(bf16[1072,128]{1,0:T(8,128)(2,1)S(1)} %attend_far.2), channel_id=1, source_target_pairs={{0,1},{1,0},{2,3},{3,2},{4,5},{5,4},{6,7},{7,6},{8,9},{9,8},{10,11... | collective-permute-start | bytes 823304 | tf_op jit(solution)/shard_map/ppermute | solution.py:557
  75.0 4.6 %collective-permute-start.9 = (bf16[1072,128]{1,0:T(8,128)(2,1)S(1)}, bf16[1072,128]{1,0:T(8,128)(2,1)S(1)}, u32[]{:S(2)}, u32[]{:S(2)}) collective-permute-start(bf16[1072,128]{1,0:T(8,128)(2,1)S(1)} %attend_far.3), channel_id=1, source_target_pairs={{0,1},{1,0},{2,3},{3,2},{4,5},{5,4},{6,7},{7,6},{8,9},{9,8},{10,11... | collective-permute-start | bytes 823304 | tf_op jit(solution)/shard_map/ppermute | solution.py:557
  78.0 8.0 %copy-start.4 = (s32[4]{0:T(128)S(1)}, s32[4]{0:T(128)}, u32[]{:S(2)}) copy-start(s32[4]{0:T(128)} %refs_0_.3) | copy-start | bytes 52
  78.0 8.0 %collective-permute-start.10 = (bf16[1072,128]{1,0:T(8,128)(2,1)S(1)}, bf16[1072,128]{1,0:T(8,128)(2,1)S(1)}, u32[]{:S(2)}, u32[]{:S(2)}) collective-permute-start(bf16[1072,128]{1,0:T(8,128)(2,1)S(1)} %get-tuple-element.53), channel_id=1, source_target_pairs={{0,2},{2,0},{1,3},{3,1},{4,6},{6,4},{5,7},{7,5},{8,10},{10,8},{9,1... | collective-permute-start | bytes 823304 | tf_op jit(solution)/shard_map/ppermute | solution.py:563
  82.5 9.3 %collective-permute-start.12 = (bf16[1072,128]{1,0:T(8,128)(2,1)S(1)}, bf16[1072,128]{1,0:T(8,128)(2,1)S(1)}, u32[]{:S(2)}, u32[]{:S(2)}) collective-permute-start(bf16[1072,128]{1,0:T(8,128)(2,1)S(1)} %get-tuple-element.56), channel_id=1, source_target_pairs={{0,2},{2,0},{1,3},{3,1},{4,6},{6,4},{5,7},{7,5},{8,10},{10,8},{9,1... | collective-permute-start | bytes 823304 | tf_op jit(solution)/shard_map/ppermute | solution.py:563
  91.9 4.0 %copy-start.1 = (bf16[1280,1024]{1,0:T(8,128)(2,1)S(1)}, bf16[1280,1024]{1,0:T(8,128)(2,1)}, u32[]{:S(2)}) copy-start(bf16[1280,1024]{1,0:T(8,128)(2,1)} %all-gather.3.cloned.1.call-done.refs_0_) | copy-start | bytes 7864324
  92.9 2.6 %collective-permute-start.13 = (bf16[256,512]{1,0:T(8,128)(2,1)S(1)}, bf16[256,512]{1,0:T(8,128)(2,1)S(1)}, u32[]{:S(2)}, u32[]{:S(2)}) collective-permute-start(bf16[256,512]{1,0:T(8,128)(2,1)S(1)} %merge_last.3.refs_3_), channel_id=1, source_target_pairs={{0,1},{1,0},{2,3},{3,2},{4,5},{5,4},{6,7},{7,6},{8,9},{9,8},{10,11... | collective-permute-start | bytes 786440 | tf_op jit(solution)/shard_map/ppermute | solution.py:573
  94.3 1.5 %collective-permute-start.11 = (bf16[256,512]{1,0:T(8,128)(2,1)S(1)}, bf16[256,512]{1,0:T(8,128)(2,1)S(1)}, u32[]{:S(2)}, u32[]{:S(2)}) collective-permute-start(bf16[256,512]{1,0:T(8,128)(2,1)S(1)} %merge_last.2.refs_1_), channel_id=1, source_target_pairs={{0,1},{1,0},{2,3},{3,2},{4,5},{5,4},{6,7},{7,6},{8,9},{9,8},{10,11... | collective-permute-start | bytes 786440 | tf_op jit(solution)/shard_map/ppermute | solution.py:573
  98.8 40.1 %all-to-all-start.1 = ((bf16[32,16,1280]{2,1,0:T(8,128)(2,1)}), bf16[32,16,1280]{2,1,0:T(8,128)(2,1)S(1)}, u32[]{:S(2)}, u32[]{:S(2)}) async-start(bf16[32,16,1280]{2,1,0:T(8,128)(2,1)} %bitcast.21), calls=%async_computation.1 | async-start | bytes 2621440 | tf_op jit(solution)/shard_map/all_to_all | solution.py:576
  (1 other events, 1.0 us)
Sparse Core Ops, SparseCore 0:
  10.9 29.8 all-gather.4
  42.6 42.8 all-gather.2

commit v3 on v2

--- a/solution.py
+++ b/solution.py
@@ -241,17 +241,16 @@
         attended_ref[:, i * HEAD_SIZE : (i + 1) * HEAD_SIZE] = head.astype(BF16)
 
 
-def project_kernel(w_ref, *refs):
-    pairs, out_ref = refs[:-1], refs[-1]
+def project_kernel(w_ref, a_ref, b_ref, *refs):
+    out_ref = refs[-1]
     devices, _, rows, width = out_ref.shape
     depth = w_ref.shape[1] // 4
-    for part in range(PARTS):
-        product = 0.0
-        for i in range(4):
-            ref, at = pairs[2 * part + i % 2], i // 2 * depth
-            weight = w_ref[:, i * depth : (i + 1) * depth]
-            product = product + score_dot(ref[:, at : at + depth], weight)
-        out_ref[:, part] = product.reshape(devices, rows, width).astype(BF16)
+    product = 0.0
+    for i in range(4):
+        ref, at = (a_ref, b_ref)[i % 2], i // 2 * depth
+        weight = w_ref[:, i * depth : (i + 1) * depth]
+        product = product + score_dot(ref[:, at : at + depth], weight)
+    out_ref[:, 0] = product.reshape(devices, rows, width).astype(BF16)
 
 
 def total_kernel(blocks, xh_ref, *refs):
@@ -408,18 +407,20 @@
     )(lengths, out, lines, got)
 
 
-def project(pairs, weight, tile=640):
-    devices = pairs[0].shape[0] // SLAB
+def project(part, a, b, weight, before, tile=640):
+    devices = a.shape[0] // SLAB
     columns, depth = weight.shape
     return call(
         project_kernel,
         "project",
-        3,
+        2,
         grid=(columns // tile,),
-        in_specs=[pl.BlockSpec((tile, depth), lambda i: (i, 0))] + [whole(a) for a in pairs],
-        out_specs=pl.BlockSpec((devices, PARTS, SLAB, tile), lambda i: (0, 0, 0, i)),
+        in_specs=[pl.BlockSpec((tile, depth), lambda i: (i, 0)), whole(a), whole(b)]
+        + [pl.BlockSpec(memory_space=pl.ANY)] * len(before),
+        out_specs=pl.BlockSpec((devices, 1, SLAB, tile), lambda i: (0, part, 0, i)),
         out_shape=jax.ShapeDtypeStruct((devices, PARTS, SLAB, columns), BF16),
-    )(weight, *pairs)
+        input_output_aliases={4: 0} if before else {},
+    )(weight, a, b, *before)
 
 
 def add_up(xh, parts, width, blocks):
@@ -555,23 +556,19 @@
         order = (far[-1],) if far else ()
         far.append(attend_far(q_all, blocks, state, part, half, order))
     far_c = [lax.ppermute(f, "c", SWAP) for f in far]
-    near, near_x, merged = [], [], []
+    near, near_x = [], []
     for part in range(PARTS):
         order = (near[-1][0],) if near else (far[-1],)
         out, lines, sent = attend_near(q_all, blocks, state, far_c[part], part, half, order)
         near.append((out, lines))
         near_x.append(lax.ppermute(sent, "xl", SWAP))
-    for part in range(PARTS - 1):
-        merged.append(
-            last_merge(part, lengths, *near[part], near_x[part], part_tokens, (near[-1][0], weight))
-        )
-    merged.append(
-        last_merge(PARTS - 1, lengths, *near[-1], near_x[-1], part_tokens, (merged[-1],))
-    )
-    pairs = []
-    for attended in merged:
-        pairs += [attended, lax.ppermute(attended, "c", SWAP)]
-    partial = project(pairs, weight)
+    partial = ()
+    for part in range(PARTS):
+        order = (near[-1][0], *partial)
+        attended = last_merge(part, lengths, *near[part], near_x[part], part_tokens, order)
+        attended_c = lax.ppermute(attended, "c", SWAP)
+        partial = (project(part, attended, attended_c, weight, partial),)
+    partial = partial[0]
     partial = partial.reshape(partial.shape[0], PARTS * SLAB, partial.shape[-1])
     received = lax.all_to_all(partial, PREFIX, split_axis=0, concat_axis=0, tiled=True)
     blocks = 2 * y_size

time: 147 us -> 150 us (1.020)
  starting transfers between devices: 32.2 us -> 34 us
  local copies, waits for them, and re-layouts: 5.63 us -> 7.37 us
  waiting for transfers between devices: 50.6 us -> 48.9 us
    all_gather x1, waiting for transfers between devices: 2.61 us -> 0.01 us  [on_device(): lax.all_gather(jnp.concatenate([here, there], axis=0), 'y', axis=0, tiled...]
    unnamed x15 -> x17, local copies, waits for them, and re-layouts: 2.64 us -> 4.39 us
    pallas_call x13 -> x14, Pallas kernels: 43.4 us -> 44.3 us  [run(): pl.pallas_call(lambda held_ref, *refs: kernel(*refs), name=name, in_specs...]
  transfers between devices with their start and end apart: 18 -> 18, of which waited for: 9 -> 7; matrix products, arithmetic and copies ran while one was open for 2% -> 2% of each run, Pallas kernels for 26% -> 26%
where the time goes in v3:
time: 150 us; the launch traced here: 149 us
  waiting for transfers between devices  48.9 us (33%)
  Pallas kernels  44.3 us (30%)
  starting transfers between devices  34 us (23%)
  between operations  13.6 us (9%)
  local copies, waits for them, and re-layouts  7.37 us (5%)
    pallas_call x14, Pallas kernels, run(): pl.pallas_call(lambda held_ref, *refs: kernel(*refs), name=name, in_specs...  44.3 us
    all_to_all x1, waiting for transfers between devices, on_device(): lax.all_to_all(partial, PREFIX, split_axis=0, concat_axis=0, tiled=True)  33.7 us
    ppermute x2, waiting for transfers between devices, on_device(): near_x.append(lax.ppermute(sent, 'xl', SWAP))  6.68 us
    all_to_all x1, starting transfers between devices, on_device(): lax.all_to_all(after(sent, both), 'z', split_axis=0, concat_axis=0, tiled...  6.45 us
    all_to_all x1, starting transfers between devices, on_device(): lax.all_to_all(partial, PREFIX, split_axis=0, concat_axis=0, tiled=True)  6.38 us
    unnamed x17, local copies, waits for them, and re-layouts  4.39 us
    ppermute x1, waiting for transfers between devices, on_device(): w_h = lax.ppermute(w_own, 'xh', SWAP)  3.6 us
    ppermute x1, starting transfers between devices, weight_of_core(): return jnp.concatenate([of_c, lax.ppermute(sent, 'c', SWAP)], axis=2)  3.33 us
  transfers between devices with their start and end apart: 18, of which 7 were waited for; matrix products, arithmetic and copies ran while one was open for 2% of the time, Pallas kernels for 26%

profile of v3, /device:TPU:1, one launch (start us, length us, event | category | flops | bytes accessed | tf_op | source)
XLA Modules:
  0.0 149.4 jit_solution(9530225976620133805)
XLA Ops:
  11.0 3.3 %collective-permute-start = (bf16[2,160,256]{2,1,0:T(8,128)(2,1)S(1)}, bf16[2,160,256]{2,1,0:T(8,128)(2,1)S(1)}, u32[]{:S(2)}, u32[]{:S(2)}) collective-permute-start(bf16[2,160,256]{2,1,0:T(8,128)(2,1)S(1)} %get-tuple-element.62), channel_id=1, source_target_pairs={{0,1},{1,0},{2,3},{3,2},{4,5},{5,4},{6,7},{7,6},{8,9},{9,8},{10,11... | collective-permute-start | bytes 491528 | tf_op jit(solution)/shard_map/ppermute | solution.py:502
  14.3 6.5 %all-to-all-start = ((bf16[8,2,128,128]{3,2,1,0:T(8,128)(2,1)}), bf16[8,2,128,128]{3,2,1,0:T(8,128)(2,1)S(1)}, u32[]{:S(2)}, u32[]{:S(2)}) async-start(bf16[8,2,128,128]{3,2,1,0:T(8,128)(2,1)} %get-tuple-element.37), calls=%async_computation | async-start | bytes 1048576 | tf_op jit(solution)/shard_map/all_to_all | solution.py:522
  23.2 1.8 %collective-permute-start.3 = (bf16[160,512]{1,0:T(8,128)(2,1)S(1)}, bf16[160,512]{1,0:T(8,128)(2,1)S(1)}, u32[]{:S(2)}, u32[]{:S(2)}) collective-permute-start(bf16[160,512]{1,0:T(8,128)(2,1)S(1)} %get-tuple-element.61), channel_id=1, source_target_pairs={{0,130},{2,128},{128,2},{130,0},{1,131},{3,129},{129,3},{131,1},{4... | collective-permute-start | bytes 491528 | tf_op jit(solution)/shard_map/ppermute | solution.py:520
  25.6 5.6 %attend_own.1 = (f32[1024,128]{1,0:T(8,128)S(1)}, f32[1024,128]{1,0:T(8,128)S(1)}) custom-call(s32[1]{0:T(128)} %constant.44.clone.1.held_ref, bf16[1024,128]{1,0:T(8,128)(2,1)S(1)} %bitcast.32, bf16[4,128,128]{2,1,0:T(8,128)(2,1)S(1)} %get-tuple-element.65.refs_1_, bf16[4,128,128]{2,1,0:T(8,128)(2,1)S(1)} %get-tuple-element.64.refs_2_, ...), custom_call_target="tpu_custom_call" | custom-call | flops 5750000128 | bytes 1 | tf_op jit(solution)/shard_map/attend_own/pallas_call | solution.py:283
  31.3 3.6 %collective-permute-done.2 = bf16[160,512]{1,0:T(8,128)(2,1)S(1)} collective-permute-done((bf16[160,512]{1,0:T(8,128)(2,1)S(1)}, bf16[160,512]{1,0:T(8,128)(2,1)S(1)}, u32[]{:S(2)}, u32[]{:S(2)}) %collective-permute-start.2) | collective-permute-done | bytes 163872 | tf_op jit(solution)/shard_map/ppermute | solution.py:519
  35.8 3.0 %all-to-all-done.refs_1_ = bf16[8,2,128,128]{3,2,1,0:T(8,128)(2,1)S(1)} async-done(((bf16[8,2,128,128]{3,2,1,0:T(8,128)(2,1)}), bf16[8,2,128,128]{3,2,1,0:T(8,128)(2,1)S(1)}, u32[]{:S(2)}, u32[]{:S(2)}) %all-to-all-start) | async-done | bytes 524320 | tf_op jit(solution)/shard_map/all_to_all | solution.py:522
  38.8 2.8 %collective-permute-start.5 = (bf16[2,896,128]{2,1,0:T(8,128)(2,1)S(1)}, bf16[2,896,128]{2,1,0:T(8,128)(2,1)S(1)}, u32[]{:S(2)}, u32[]{:S(2)}) collective-permute-start(bf16[2,896,128]{2,1,0:T(8,128)(2,1)S(1)} %unpack_heads.1.refs_2_.refs_1_), channel_id=1, source_target_pairs={{0,96},{32,0},{64,32},{96,64},{1,97},{33,1},{65,33},{97,65},{2,98}... | collective-permute-start | bytes 1376264 | tf_op jit(solution)/shard_map/ppermute | solution.py:536
  43.0 9.2 %attend_first.1 = (f32[4096,128]{1,0:T(8,128)S(1)}, f32[4096,128]{1,0:T(8,128)S(1)}) custom-call(s32[1]{0:T(128)} %constant.44.clone.1.held_ref, bf16[4096,128]{1,0:T(8,128)(2,1)S(1)} %bitcast.34, bf16[2,512,128]{2,1,0:T(8,128)(2,1)S(1)} %get-tuple-element.31.refs_3_.refs_1_, bf16[2,896,128]{2,1,0:T(8,128)(2,1)S(1)} %unpack_heads.1.refs_2_.refs_1_, ...), custom_call_target="tpu_custom_call" | custom-call | flops 12650000384 | bytes 1 | tf_op jit(solution)/shard_map/attend_first/pallas_call | solution.py:283
  52.2 2.7 %collective-permute-start.7 = (bf16[896,128]{1,0:T(8,128)(2,1)S(1)}, bf16[896,128]{1,0:T(8,128)(2,1)S(1)}, u32[]{:S(2)}, u32[]{:S(2)}) collective-permute-start(bf16[896,128]{1,0:T(8,128)(2,1)S(1)} %slice_bitcast_fusion), channel_id=1, source_target_pairs={{0,96},{32,0},{64,32},{96,64},{1,97},{33,1},{65,33},{97,65},{2,98}... | collective-permute-start | bytes 688136 | tf_op jit(solution)/shard_map/ppermute | solution.py:550
  55.3 10.8 %attend_more.1 = (f32[4096,128]{1,0:T(8,128)S(1)}, f32[4096,128]{1,0:T(8,128)S(1)}) custom-call(s32[1]{0:T(128)} %constant.44.clone.1.held_ref, bf16[4096,128]{1,0:T(8,128)(2,1)S(1)} %bitcast.35, bf16[2,896,128]{2,1,0:T(8,128)(2,1)S(1)} %unpack_heads.1.refs_2_.refs_1_, bf16[2,896,128]{2,1,0:T(8,128)(2,1)S(1)} %collective-permute-done.4.refs_2_, ...), custom_call_target="tpu_custom_call" | custom-call | flops 24149999616 | bytes 1 | tf_op jit(solution)/shard_map/attend_more/pallas_call | solution.py:283
  66.8 2.5 %attend_far.2 = bf16[1072,128]{1,0:T(8,128)(2,1)S(1)} custom-call(s32[1]{0:T(128)} %constant.44.clone.1.held_ref, bf16[4096,128]{1,0:T(8,128)(2,1)S(1)} %bitcast.36, f32[4096,128]{1,0:T(8,128)S(1)} %get-tuple-element.42.refs_1_, f32[4096,128]{1,0:T(8,128)S(1)} %get-tuple-element.43.refs_2_, bf16[2,896,128]{2,1,0:T(8,128)(2,1)S(1)} %collective-permute-done.5.refs_3_, ...), custom_call_target="tpu_custom_call" | custom-call | flops 2300000000 | bytes 1 | tf_op jit(solution)/shard_map/attend_far/pallas_call | solution.py:283
  69.4 3.0 %collective-permute-start.8 = (bf16[1072,128]{1,0:T(8,128)(2,1)S(1)}, bf16[1072,128]{1,0:T(8,128)(2,1)S(1)}, u32[]{:S(2)}, u32[]{:S(2)}) collective-permute-start(bf16[1072,128]{1,0:T(8,128)(2,1)S(1)} %attend_far.2), channel_id=1, source_target_pairs={{0,1},{1,0},{2,3},{3,2},{4,5},{5,4},{6,7},{7,6},{8,9},{9,8},{10,11... | collective-permute-start | bytes 823304 | tf_op jit(solution)/shard_map/ppermute | solution.py:558
  72.4 2.5 %attend_far.3 = bf16[1072,128]{1,0:T(8,128)(2,1)S(1)} custom-call(s32[1]{0:T(128)} %constant.44.clone.1.held_ref, bf16[4096,128]{1,0:T(8,128)(2,1)S(1)} %bitcast.37, f32[4096,128]{1,0:T(8,128)S(1)} %get-tuple-element.42.refs_1_, f32[4096,128]{1,0:T(8,128)S(1)} %get-tuple-element.43.refs_2_, bf16[2,896,128]{2,1,0:T(8,128)(2,1)S(1)} %collective-permute-done.5.refs_3_, ...), custom_call_target="tpu_custom_call" | custom-call | flops 2300000000 | bytes 1 | tf_op jit(solution)/shard_map/attend_far/pallas_call | solution.py:283
  75.1 3.0 %attend_near.2 = (f32[1024,128]{1,0:T(8,128)S(1)}, f32[16,128]{1,0:T(8,128)S(1)}, bf16[1072,128]{1,0:T(8,128)(2,1)S(1)}) custom-call(s32[1]{0:T(128)} %constant.44.clone.1.held_ref, bf16[4096,128]{1,0:T(8,128)(2,1)S(1)} %bitcast.38, f32[4096,128]{1,0:T(8,128)S(1)} %get-tuple-element.42.refs_1_, f32[4096,128]{1,0:T(8,128)S(1)} %get-tuple-element.43.refs_2_, ...), custom_call_target="tpu_custom_call" | custom-call | flops 2300000000 | bytes 1 | tf_op jit(solution)/shard_map/attend_near/pallas_call | solution.py:283
  78.0 1.5 %collective-permute-start.10 = (bf16[1072,128]{1,0:T(8,128)(2,1)S(1)}, bf16[1072,128]{1,0:T(8,128)(2,1)S(1)}, u32[]{:S(2)}, u32[]{:S(2)}) collective-permute-start(bf16[1072,128]{1,0:T(8,128)(2,1)S(1)} %get-tuple-element.53), channel_id=1, source_target_pairs={{0,2},{2,0},{1,3},{3,1},{4,6},{6,4},{5,7},{7,5},{8,10},{10,8},{9,1... | collective-permute-start | bytes 823304 | tf_op jit(solution)/shard_map/ppermute | solution.py:564
  79.5 3.0 %attend_near.3 = (f32[1024,128]{1,0:T(8,128)S(1)}, f32[16,128]{1,0:T(8,128)S(1)}, bf16[1072,128]{1,0:T(8,128)(2,1)S(1)}) custom-call(s32[1]{0:T(128)} %constant.44.clone.1.held_ref, bf16[4096,128]{1,0:T(8,128)(2,1)S(1)} %bitcast.39, f32[4096,128]{1,0:T(8,128)S(1)} %get-tuple-element.42.refs_1_, f32[4096,128]{1,0:T(8,128)S(1)} %get-tuple-element.43.refs_2_, ...), custom_call_target="tpu_custom_call" | custom-call | flops 2300000000 | bytes 1 | tf_op jit(solution)/shard_map/attend_near/pallas_call | solution.py:283
  82.5 3.5 %collective-permute-done.10.refs_3_ = bf16[1072,128]{1,0:T(8,128)(2,1)S(1)} collective-permute-done((bf16[1072,128]{1,0:T(8,128)(2,1)S(1)}, bf16[1072,128]{1,0:T(8,128)(2,1)S(1)}, u32[]{:S(2)}, u32[]{:S(2)}) %collective-permute-start.10) | collective-permute-done | bytes 274464 | tf_op jit(solution)/shard_map/ppermute | solution.py:564
  87.0 1.4 collective-permute-start.11
  89.7 1.7 %copy-done.1 = bf16[1280,1024]{1,0:T(8,128)(2,1)S(1)} copy-done((bf16[1280,1024]{1,0:T(8,128)(2,1)S(1)}, bf16[1280,1024]{1,0:T(8,128)(2,1)}, u32[]{:S(2)}) %copy-start.1) | copy-done | bytes 2621464
  91.4 1.9 %project.2.refs_3_ = bf16[32,2,8,1280]{3,2,1,0:T(8,128)(2,1)} custom-call(s32[1]{0:T(128)} %constant.44.clone.1.held_ref, bf16[1280,1024]{1,0:T(8,128)(2,1)S(1)} %copy-done.1, bf16[256,512]{1,0:T(8,128)(2,1)S(1)} %merge_last.2.refs_1_, bf16[256,512]{1,0:T(8,128)(2,1)S(1)} %collective-permute-done.11.refs_2_), custom_call_target="tpu_custom_call" | custom-call | flops 2300000000 | bytes 1 | tf_op jit(solution)/shard_map/project/pallas_call | solution.py:283
  93.3 3.2 %collective-permute-done.12.refs_3_ = bf16[1072,128]{1,0:T(8,128)(2,1)S(1)} collective-permute-done((bf16[1072,128]{1,0:T(8,128)(2,1)S(1)}, bf16[1072,128]{1,0:T(8,128)(2,1)S(1)}, u32[]{:S(2)}, u32[]{:S(2)}) %collective-permute-start.12) | collective-permute-done | bytes 274464 | tf_op jit(solution)/shard_map/ppermute | solution.py:564
  99.7 1.9 %project.3 = bf16[32,2,8,1280]{3,2,1,0:T(8,128)(2,1)} custom-call(s32[1]{0:T(128)} %constant.44.clone.1.held_ref, bf16[1280,1024]{1,0:T(8,128)(2,1)S(1)} %copy-done.2, bf16[256,512]{1,0:T(8,128)(2,1)S(1)} %merge_last.3.refs_1_, bf16[256,512]{1,0:T(8,128)(2,1)S(1)} %collective-permute-done.13.refs_2_, ...), custom_call_target="tpu_custom_call", output_to_operand_aliasing={{}: (4, {})} | custom-call | flops 2300000000 | bytes 1 | tf_op jit(solution)/shard_map/project/pallas_call | solution.py:283
  101.6 6.4 %all-to-all-start.1 = ((bf16[32,16,1280]{2,1,0:T(8,128)(2,1)}), bf16[32,16,1280]{2,1,0:T(8,128)(2,1)S(1)}, u32[]{:S(2)}, u32[]{:S(2)}) async-start(bf16[32,16,1280]{2,1,0:T(8,128)(2,1)} %bitcast.21), calls=%async_computation.1 | async-start | bytes 2621440 | tf_op jit(solution)/shard_map/all_to_all | solution.py:573
  108.0 33.7 %all-to-all-done.1.refs_1_ = bf16[32,16,1280]{2,1,0:T(8,128)(2,1)S(1)} async-done(((bf16[32,16,1280]{2,1,0:T(8,128)(2,1)}), bf16[32,16,1280]{2,1,0:T(8,128)(2,1)S(1)}, u32[]{:S(2)}, u32[]{:S(2)}) %all-to-all-start.1) | async-done | bytes 1310752 | tf_op jit(solution)/shard_map/all_to_all | solution.py:573
  (54 shorter events, 17.2 us)
Async XLA Ops:
  6.5 35.1 %all-gather.5.cloned.1.call-start = ((), (), s32[]{:S(2)}) async-start(), calls=%async_computation.3 | async-start | bytes 1310720 | tf_op jit(solution)/shard_map/all_gather | solution.py:526
  6.5 1.2 copy-start.3
  9.0 1.8 %copy-start.6 = (bf16[256,640]{1,0:T(8,128)(2,1)S(1)}, bf16[256,640]{1,0:T(8,128)(2,1)}, u32[]{:S(2)}) copy-start(bf16[256,640]{1,0:T(8,128)(2,1)} %param.13) | copy-start | bytes 983044
  11.0 14.7 %copy-start = (bf16[32,2,8,2,128]{4,2,0,3,1:T(8,128)(2,1)S(1)}, bf16[32,2,8,2,128]{4,2,0,3,1:T(8,128)(2,1)}, u32[]{:S(2)}) copy-start(bf16[32,2,8,2,128]{4,2,0,3,1:T(8,128)(2,1)} %copy.15) | copy-start | bytes 786436
  11.0 10.8 %collective-permute-start = (bf16[2,160,256]{2,1,0:T(8,128)(2,1)S(1)}, bf16[2,160,256]{2,1,0:T(8,128)(2,1)S(1)}, u32[]{:S(2)}, u32[]{:S(2)}) collective-permute-start(bf16[2,160,256]{2,1,0:T(8,128)(2,1)S(1)} %get-tuple-element.62), channel_id=1, source_target_pairs={{0,1},{1,0},{2,3},{3,2},{4,5},{5,4},{6,7},{7,6},{8,9},{9,8},{10,11... | collective-permute-start | bytes 491528 | tf_op jit(solution)/shard_map/ppermute | solution.py:502
  14.3 24.5 %all-to-all-start = ((bf16[8,2,128,128]{3,2,1,0:T(8,128)(2,1)}), bf16[8,2,128,128]{3,2,1,0:T(8,128)(2,1)S(1)}, u32[]{:S(2)}, u32[]{:S(2)}) async-start(bf16[8,2,128,128]{3,2,1,0:T(8,128)(2,1)} %get-tuple-element.37), calls=%async_computation | async-start | bytes 1048576 | tf_op jit(solution)/shard_map/all_to_all | solution.py:522
  20.8 68.9 %all-gather.3.cloned.1.call-start = ((), (), s32[]{:S(2)}) async-start(), calls=%async_computation.2 | async-start | bytes 3276800 | tf_op jit(solution)/shard_map/all_gather | solution.py:539
  21.9 9.4 %collective-permute-start.1 = (bf16[160,512]{1,0:T(8,128)(2,1)S(1)}, bf16[160,512]{1,0:T(8,128)(2,1)S(1)}, u32[]{:S(2)}, u32[]{:S(2)}) collective-permute-start(bf16[160,512]{1,0:T(8,128)(2,1)S(1)} %get-tuple-element.61), channel_id=1, source_target_pairs={{0,2},{2,0},{1,3},{3,1},{4,6},{6,4},{5,7},{7,5},{8,10},{10,8},{9,1... | collective-permute-start | bytes 491528 | tf_op jit(solution)/shard_map/ppermute | solution.py:518
  23.2 11.7 %collective-permute-start.3 = (bf16[160,512]{1,0:T(8,128)(2,1)S(1)}, bf16[160,512]{1,0:T(8,128)(2,1)S(1)}, u32[]{:S(2)}, u32[]{:S(2)}) collective-permute-start(bf16[160,512]{1,0:T(8,128)(2,1)S(1)} %get-tuple-element.61), channel_id=1, source_target_pairs={{0,130},{2,128},{128,2},{130,0},{1,131},{3,129},{129,3},{131,1},{4... | collective-permute-start | bytes 491528 | tf_op jit(solution)/shard_map/ppermute | solution.py:520
  25.0 9.9 %collective-permute-start.2 = (bf16[160,512]{1,0:T(8,128)(2,1)S(1)}, bf16[160,512]{1,0:T(8,128)(2,1)S(1)}, u32[]{:S(2)}, u32[]{:S(2)}) collective-permute-start(bf16[160,512]{1,0:T(8,128)(2,1)S(1)} %get-tuple-element.60), channel_id=1, source_target_pairs={{0,128},{128,0},{1,129},{129,1},{2,130},{130,2},{3,131},{131,3},{4... | collective-permute-start | bytes 491528 | tf_op jit(solution)/shard_map/ppermute | solution.py:519
  38.8 13.3 %collective-permute-start.5 = (bf16[2,896,128]{2,1,0:T(8,128)(2,1)S(1)}, bf16[2,896,128]{2,1,0:T(8,128)(2,1)S(1)}, u32[]{:S(2)}, u32[]{:S(2)}) collective-permute-start(bf16[2,896,128]{2,1,0:T(8,128)(2,1)S(1)} %unpack_heads.1.refs_2_.refs_1_), channel_id=1, source_target_pairs={{0,96},{32,0},{64,32},{96,64},{1,97},{33,1},{65,33},{97,65},{2,98}... | collective-permute-start | bytes 1376264 | tf_op jit(solution)/shard_map/ppermute | solution.py:536
  41.7 13.3 %collective-permute-start.4 = (bf16[2,896,128]{2,1,0:T(8,128)(2,1)S(1)}, bf16[2,896,128]{2,1,0:T(8,128)(2,1)S(1)}, u32[]{:S(2)}, u32[]{:S(2)}) collective-permute-start(bf16[2,896,128]{2,1,0:T(8,128)(2,1)S(1)} %unpack_heads.1.refs_2_.refs_1_), channel_id=1, source_target_pairs={{0,32},{32,64},{64,96},{96,0},{1,33},{33,65},{65,97},{97,1},{2,34}... | collective-permute-start | bytes 1376264 | tf_op jit(solution)/shard_map/ppermute | solution.py:535
  52.2 13.9 %collective-permute-start.7 = (bf16[896,128]{1,0:T(8,128)(2,1)S(1)}, bf16[896,128]{1,0:T(8,128)(2,1)S(1)}, u32[]{:S(2)}, u32[]{:S(2)}) collective-permute-start(bf16[896,128]{1,0:T(8,128)(2,1)S(1)} %slice_bitcast_fusion), channel_id=1, source_target_pairs={{0,96},{32,0},{64,32},{96,64},{1,97},{33,1},{65,33},{97,65},{2,98}... | collective-permute-start | bytes 688136 | tf_op jit(solution)/shard_map/ppermute | solution.py:550
  55.0 11.9 %collective-permute-start.6 = (bf16[896,128]{1,0:T(8,128)(2,1)S(1)}, bf16[896,128]{1,0:T(8,128)(2,1)S(1)}, u32[]{:S(2)}, u32[]{:S(2)}) collective-permute-start(bf16[896,128]{1,0:T(8,128)(2,1)S(1)} %slice_bitcast_fusion.1), channel_id=1, source_target_pairs={{0,32},{32,64},{64,96},{96,0},{1,33},{33,65},{65,97},{97,1},{2,34}... | collective-permute-start | bytes 688136 | tf_op jit(solution)/shard_map/ppermute | solution.py:549
  69.4 5.7 %collective-permute-start.8 = (bf16[1072,128]{1,0:T(8,128)(2,1)S(1)}, bf16[1072,128]{1,0:T(8,128)(2,1)S(1)}, u32[]{:S(2)}, u32[]{:S(2)}) collective-permute-start(bf16[1072,128]{1,0:T(8,128)(2,1)S(1)} %attend_far.2), channel_id=1, source_target_pairs={{0,1},{1,0},{2,3},{3,2},{4,5},{5,4},{6,7},{7,6},{8,9},{9,8},{10,11... | collective-permute-start | bytes 823304 | tf_op jit(solution)/shard_map/ppermute | solution.py:558
  75.0 4.6 %collective-permute-start.9 = (bf16[1072,128]{1,0:T(8,128)(2,1)S(1)}, bf16[1072,128]{1,0:T(8,128)(2,1)S(1)}, u32[]{:S(2)}, u32[]{:S(2)}) collective-permute-start(bf16[1072,128]{1,0:T(8,128)(2,1)S(1)} %attend_far.3), channel_id=1, source_target_pairs={{0,1},{1,0},{2,3},{3,2},{4,5},{5,4},{6,7},{7,6},{8,9},{9,8},{10,11... | collective-permute-start | bytes 823304 | tf_op jit(solution)/shard_map/ppermute | solution.py:558
  78.0 7.9 %collective-permute-start.10 = (bf16[1072,128]{1,0:T(8,128)(2,1)S(1)}, bf16[1072,128]{1,0:T(8,128)(2,1)S(1)}, u32[]{:S(2)}, u32[]{:S(2)}) collective-permute-start(bf16[1072,128]{1,0:T(8,128)(2,1)S(1)} %get-tuple-element.53), channel_id=1, source_target_pairs={{0,2},{2,0},{1,3},{3,1},{4,6},{6,4},{5,7},{7,5},{8,10},{10,8},{9,1... | collective-permute-start | bytes 823304 | tf_op jit(solution)/shard_map/ppermute | solution.py:564
  79.5 6.4 %copy-start.5 = (s32[4]{0:T(128)S(1)}, s32[4]{0:T(128)}, u32[]{:S(2)}) copy-start(s32[4]{0:T(128)} %refs_0_.3) | copy-start | bytes 52
  87.0 2.7 %collective-permute-start.11 = (bf16[256,512]{1,0:T(8,128)(2,1)S(1)}, bf16[256,512]{1,0:T(8,128)(2,1)S(1)}, u32[]{:S(2)}, u32[]{:S(2)}) collective-permute-start(bf16[256,512]{1,0:T(8,128)(2,1)S(1)} %merge_last.2.refs_1_), channel_id=1, source_target_pairs={{0,1},{1,0},{2,3},{3,2},{4,5},{5,4},{6,7},{7,6},{8,9},{9,8},{10,11... | collective-permute-start | bytes 786440 | tf_op jit(solution)/shard_map/ppermute | solution.py:569
  88.4 8.1 %collective-permute-start.12 = (bf16[1072,128]{1,0:T(8,128)(2,1)S(1)}, bf16[1072,128]{1,0:T(8,128)(2,1)S(1)}, u32[]{:S(2)}, u32[]{:S(2)}) collective-permute-start(bf16[1072,128]{1,0:T(8,128)(2,1)S(1)} %get-tuple-element.56), channel_id=1, source_target_pairs={{0,2},{2,0},{1,3},{3,1},{4,6},{6,4},{5,7},{7,5},{8,10},{10,8},{9,1... | collective-permute-start | bytes 823304 | tf_op jit(solution)/shard_map/ppermute | solution.py:564
  89.7 1.7 %copy-start.1 = (bf16[1280,1024]{1,0:T(8,128)(2,1)S(1)}, bf16[1280,1024]{1,0:T(8,128)(2,1)}, u32[]{:S(2)}) copy-start(bf16[1280,1024]{1,0:T(8,128)(2,1)} %all-gather.3.cloned.1.call-done.refs_0_) | copy-start | bytes 7864324
  96.5 3.1 %copy-start.2 = (bf16[1280,1024]{1,0:T(8,128)(2,1)S(1)}, bf16[1280,1024]{1,0:T(8,128)(2,1)}, u32[]{:S(2)}) copy-start(bf16[1280,1024]{1,0:T(8,128)(2,1)} %all-gather.3.cloned.1.call-done.refs_0_) | copy-start | bytes 7864324
  97.5 2.1 %collective-permute-start.13 = (bf16[256,512]{1,0:T(8,128)(2,1)S(1)}, bf16[256,512]{1,0:T(8,128)(2,1)S(1)}, u32[]{:S(2)}, u32[]{:S(2)}) collective-permute-start(bf16[256,512]{1,0:T(8,128)(2,1)S(1)} %merge_last.3.refs_1_), channel_id=1, source_target_pairs={{0,1},{1,0},{2,3},{3,2},{4,5},{5,4},{6,7},{7,6},{8,9},{9,8},{10,11... | collective-permute-start | bytes 786440 | tf_op jit(solution)/shard_map/ppermute | solution.py:569
  101.6 40.1 %all-to-all-start.1 = ((bf16[32,16,1280]{2,1,0:T(8,128)(2,1)}), bf16[32,16,1280]{2,1,0:T(8,128)(2,1)S(1)}, u32[]{:S(2)}, u32[]{:S(2)}) async-start(bf16[32,16,1280]{2,1,0:T(8,128)(2,1)} %bitcast.21), calls=%async_computation.1 | async-start | bytes 2621440 | tf_op jit(solution)/shard_map/all_to_all | solution.py:573
  (2 other events, 2.2 us)
Sparse Core Ops, SparseCore 0:
  10.9 29.8 all-gather.4
  42.6 42.8 all-gather.2
